TPU v7x, 32 devices: a whole 2x2x4 slice. The times are simulated.
32 devices in a mesh: gz: 4 (over y, x), xy: 8 (over z, core).
Axes of the slice: x: 2, y: 2, z: 4, core: 2. Of those that a mesh axis runs over, the one named last changes fastest.
Arguments:
- u_wind: bfloat16 [4, 2048, 2048], P('gz', 'xy'), may hold values from -6 to 6
- v_wind: bfloat16 [4, 2048, 2048], P('gz', 'xy'), may hold values from -6 to 6
- w_wind: bfloat16 [4, 2048, 2048], P('gz', 'xy'), may hold values from -4 to 4
- scalar: bfloat16 [4, 2048, 2048], P('gz', 'xy'), may hold values from -6 to 6
- heights: int32 [2048, 2048], P('xy'), may hold values from 0 to 4
- wall_class: int32 [2048, 2048], P('xy'), may hold values from 0 to 7
- wall_area: float32 [8], replicated, may hold values from 0.1 to 2
- wall_heat: float32 [8], replicated, may hold values from 0.1 to 1
Outputs:
- tendency: bfloat16 [4, 2048, 2048], P('gz', 'xy')
- pressure: float32 [4, 2048, 2048], P('gz', 'xy')
Inputs may be any that keep to these rules, and one draw needn't show every extreme that they name: A cell of level l lies in the building layer of its column where l < heights. `wall_class`: class index of each column into wall_area and wall_heat.
All inputs are finite; a program needn't handle non-finite values.
Results may differ from a plain program's by a relative error of at most 0.0039.
Values may be sent and summed in bfloat16 or wider, within the bound.
A program may use at most 192 MiB of HBM per device.

v0:
```python
from functools import partial
import math

import jax
import jax.numpy as jnp
from jax import lax
from jax.sharding import PartitionSpec as P

KX = 640
KY = 640
BAND = 64


GRID_STEP = 2.5
LEVEL_STEP = 2.5
DRAG_STEP = 0.5
GUST_FLOOR = 0.25


def for_sending(array):

    def short(part):
        return part.astype(jnp.bfloat16) if part.dtype == jnp.float32 else part

    return jax.tree.map(short, array)


def from_behind(array, axis, by):
    size = lax.axis_size(axis)
    pairs = [(i, i + by) for i in range(size) if 0 <= i + by < size]
    return lax.ppermute(array, axis, pairs)


def padded_2(array, sides, width):
    for axis, dim in sides:
        size, length = (lax.axis_size(axis), array.shape[dim])
        up = [(i, (i + 1) % size) for i in range(size - 1)]
        down = [(j, i) for i, j in up]
        last = lax.slice_in_dim(array, length - width, length, axis=dim)
        initial = lax.slice_in_dim(array, 0, width, axis=dim)
        before = lax.ppermute(last, axis, up)
        after = lax.ppermute(initial, axis, down)
        array = jnp.concatenate([before, array, after], axis=dim)
    return array


def signed_index(count, positions):
    return jnp.where(positions < count // 2, positions, positions - count)


def wave_number(count, positions):
    return 2.0 * math.pi / (count * GRID_STEP) * positions.astype(jnp.float32)


def twiddles(row_index, col_index, period, sign):
    products = row_index[:, None] * col_index[None, :] % period
    phase_angle = 2.0 * math.pi * sign / period * products.astype(jnp.float32)
    return (jnp.cos(phase_angle), jnp.sin(phase_angle))


def contract(pattern, real_part, imag_part, cosines, sines):
    multiply = partial(
        jnp.einsum, pattern, precision=lax.Precision.HIGHEST, preferred_element_type=jnp.float32
    )
    if imag_part is None:
        return (multiply(real_part, cosines), multiply(real_part, sines))
    return (
        multiply(real_part, cosines) - multiply(imag_part, sines),
        multiply(real_part, sines) + multiply(imag_part, cosines),
    )


def transform(real_part, imag_part, sign, trailing):
    full_shape = real_part.shape
    axis_position = len(full_shape) - 1 - trailing
    length = full_shape[axis_position]
    first_factor = 2 ** ((length.bit_length() - 1) // 2)
    second_factor = length // first_factor
    split_shape = (
        full_shape[:axis_position] + (first_factor, second_factor) + full_shape[axis_position + 1 :]
    )
    tail_letters = "m" * trailing
    outer_index = jnp.arange(first_factor, dtype=jnp.int32)
    inner_index = jnp.arange(second_factor, dtype=jnp.int32)
    cos_first, sin_first = twiddles(outer_index, outer_index, first_factor, sign)
    cos_twist, sin_twist = twiddles(outer_index, inner_index, length, sign)
    cos_second, sin_second = twiddles(inner_index, inner_index, second_factor, sign)
    lifted = None
    if imag_part is not None:
        lifted = imag_part.reshape(split_shape)
    section_real, section_imag = contract(
        "...ab" + tail_letters + ",ac->...cb" + tail_letters,
        real_part.reshape(split_shape),
        lifted,
        cos_first,
        sin_first,
    )
    twist_shape = (first_factor, second_factor) + (1,) * trailing
    cos_twist = cos_twist.reshape(twist_shape)
    sin_twist = sin_twist.reshape(twist_shape)
    twisted_real = section_real * cos_twist - section_imag * sin_twist
    twisted_imag = section_real * sin_twist + section_imag * cos_twist
    final_real, final_imag = contract(
        "...cb" + tail_letters + ",bd->...cd" + tail_letters,
        twisted_real,
        twisted_imag,
        cos_second,
        sin_second,
    )
    final_real = jnp.swapaxes(final_real, axis_position, axis_position + 1).reshape(full_shape)
    final_imag = jnp.swapaxes(final_imag, axis_position, axis_position + 1).reshape(full_shape)
    return (final_real, final_imag)


def pass_upward(stacked):
    return from_behind(for_sending(stacked), "gz", 1).astype(stacked.dtype)


def pass_downward(stacked):
    return from_behind(for_sending(stacked), "gz", -1).astype(stacked.dtype)


def per_device(u_wind, v_wind, w_wind, scalar, heights, wall_class, wall_area, wall_heat):
    level_count, row_count, column_count = u_wind.shape
    strips = lax.axis_size("xy")
    groups = lax.axis_size("gz")
    total_rows = row_count * strips
    first_level = lax.axis_index("gz") * level_count
    levels = first_level + jnp.arange(level_count, dtype=jnp.int32)
    inside = (levels[:, None, None] < heights[None]).astype(jnp.float32)
    class_ids = jnp.arange(wall_area.shape[0], dtype=jnp.int32)
    class_match = wall_class[None] == class_ids[:, None, None]
    wall_density = jnp.sum(jnp.where(class_match, wall_area[:, None, None], 0.0), axis=0)
    wall_source = jnp.sum(jnp.where(class_match, wall_heat[:, None, None], 0.0), axis=0)
    east_wind = u_wind.astype(jnp.float32)
    north_wind = v_wind.astype(jnp.float32)
    tracer = scalar.astype(jnp.float32)
    wind_speed = jnp.sqrt(east_wind * east_wind + north_wind * north_wind + GUST_FLOOR)
    drag_factor = 1.0 + DRAG_STEP * wall_density[None] * inside * wind_speed
    east_star = east_wind / drag_factor
    north_star = north_wind / drag_factor
    padded = padded_2(jnp.stack([w_wind, scalar]), (("gz", 1),), 1).astype(jnp.float32)
    vertical_wind = padded[0, 1:-1]
    w_above = padded[0, 2:]
    c_above = padded[1, 2:]
    c_below = padded[1, :-2]
    vertical = (
        w_above * (c_above + tracer) * 0.5 - vertical_wind * (tracer + c_below) * 0.5
    ) / LEVEL_STEP
    stretch = (w_above - vertical_wind) / LEVEL_STEP
    fields = jnp.stack([east_star, north_star, east_star * tracer, north_star * tracer, stretch])
    spec_real, spec_imag = transform(fields, None, -1.0, 0)
    column_signed = signed_index(column_count, jnp.arange(column_count, dtype=jnp.int32))
    wave_y = wave_number(column_count, column_signed)
    keep_y = (column_signed >= -KY) & (column_signed < KY)
    sent_real = jnp.where(
        keep_y,
        jnp.stack(
            [
                spec_real[0],
                spec_real[4] - wave_y * spec_imag[1],
                spec_real[2],
                -wave_y * spec_imag[3],
            ]
        ),
        0.0,
    )
    sent_imag = jnp.where(
        keep_y,
        jnp.stack(
            [
                spec_imag[0],
                spec_imag[4] + wave_y * spec_real[1],
                spec_imag[2],
                wave_y * spec_real[3],
            ]
        ),
        0.0,
    )
    share = 2 * KY // strips
    narrow_real = jnp.concatenate(
        [sent_real[..., :KY], sent_real[..., column_count - KY :]], axis=3
    )
    narrow_imag = jnp.concatenate(
        [sent_imag[..., :KY], sent_imag[..., column_count - KY :]], axis=3
    )
    spectra_pair = (
        lax.all_to_all(narrow_real, "xy", split_axis=3, concat_axis=2, tiled=True),
        lax.all_to_all(narrow_imag, "xy", split_axis=3, concat_axis=2, tiled=True),
    )
    out_real, out_imag = transform(spectra_pair[0], spectra_pair[1], -1.0, 1)
    local_columns = lax.axis_index("xy") * share + jnp.arange(share, dtype=jnp.int32)
    local_signed = jnp.where(local_columns < KY, local_columns, local_columns - 2 * KY)
    wave_local = wave_number(column_count, local_signed)
    row_signed = signed_index(total_rows, jnp.arange(total_rows, dtype=jnp.int32))
    wave_x = wave_number(total_rows, row_signed)[:, None]
    keep_x = ((row_signed >= -KX) & (row_signed < KX))[:, None]
    rhs_real = out_real[1] - wave_x * out_imag[0]
    rhs_imag = out_imag[1] + wave_x * out_real[0]
    div_real = jnp.where(keep_x, out_real[3] - wave_x * out_imag[2], 0.0)
    div_imag = jnp.where(keep_x, out_imag[3] + wave_x * out_real[2], 0.0)
    band_real = jnp.concatenate([rhs_real[:, :BAND], rhs_real[:, total_rows - BAND :]], axis=1)
    band_imag = jnp.concatenate([rhs_imag[:, :BAND], rhs_imag[:, total_rows - BAND :]], axis=1)
    wave_band = jnp.concatenate([wave_x[:BAND], wave_x[total_rows - BAND :]], axis=0)
    coupling = 1.0 / (LEVEL_STEP * LEVEL_STEP)
    diagonal = -2.0 * coupling - (wave_band * wave_band + (wave_local * wave_local)[None, :])
    upper_ratio = jnp.zeros_like(diagonal)
    pivots = []
    ratios = []
    for level_index in range(groups * level_count):
        pivot_value = diagonal - coupling * upper_ratio
        upper_ratio = coupling / pivot_value
        pivots.append(pivot_value)
        ratios.append(upper_ratio)
    own_pivots = lax.dynamic_slice_in_dim(jnp.stack(pivots), first_level, level_count, 0)
    own_ratios = lax.dynamic_slice_in_dim(jnp.stack(ratios), first_level, level_count, 0)
    carry_gain = jnp.ones_like(diagonal)
    carry_real = jnp.zeros_like(diagonal)
    carry_imag = jnp.zeros_like(diagonal)
    level_index = 0
    step_gain = -coupling / own_pivots[level_index]
    carry_gain = step_gain * carry_gain
    carry_real = step_gain * carry_real + band_real[level_index] / own_pivots[level_index]
    carry_imag = step_gain * carry_imag + band_imag[level_index] / own_pivots[level_index]
    incoming = jnp.zeros((2,) + diagonal.shape, jnp.float32)
    for step_index in range(groups - 1):
        incoming = pass_upward(
            jnp.stack(
                [carry_gain * incoming[0] + carry_real, carry_gain * incoming[1] + carry_imag]
            )
        )
    below_real, below_imag = (incoming[0], incoming[1])
    level_index = 0
    step_gain = -coupling / own_pivots[level_index]
    below_real = step_gain * below_real + band_real[level_index] / own_pivots[level_index]
    below_imag = step_gain * below_imag + band_imag[level_index] / own_pivots[level_index]
    reduced_real = [below_real]
    reduced_imag = [below_imag]
    back_gain = jnp.ones_like(diagonal)
    back_real = jnp.zeros_like(diagonal)
    back_imag = jnp.zeros_like(diagonal)
    for level_index in reversed(range(level_count)):
        step_gain = -own_ratios[level_index]
        back_gain = step_gain * back_gain
        back_real = step_gain * back_real + reduced_real[level_index]
        back_imag = step_gain * back_imag + reduced_imag[level_index]
    incoming = jnp.zeros((2,) + diagonal.shape, jnp.float32)
    for step_index in range(groups - 1):
        incoming = pass_downward(
            jnp.stack([back_gain * incoming[0] + back_real, back_gain * incoming[1] + back_imag])
        )
    above_real, above_imag = (incoming[0], incoming[1])
    solved_real = [None] * level_count
    solved_imag = [None] * level_count
    for level_index in reversed(range(level_count)):
        above_real = reduced_real[level_index] - own_ratios[level_index] * above_real
        above_imag = reduced_imag[level_index] - own_ratios[level_index] * above_imag
        solved_real[level_index] = above_real
        solved_imag[level_index] = above_imag
    solved_real = jnp.stack(solved_real)
    solved_imag = jnp.stack(solved_imag)
    band_positions = jnp.concatenate(
        [
            jnp.arange(BAND, dtype=jnp.int32),
            jnp.arange(total_rows - BAND, total_rows, dtype=jnp.int32),
        ]
    )
    cos_band, sin_band = twiddles(
        jnp.arange(total_rows, dtype=jnp.int32), band_positions, total_rows, 1.0
    )
    press_real, press_imag = contract("lbc,sb->lsc", solved_real, solved_imag, cos_band, sin_band)
    div_back_real, div_back_imag = transform(div_real, div_imag, 1.0, 1)
    inverse_real = jnp.stack([div_back_real, press_real])
    inverse_imag = jnp.stack([div_back_imag, press_imag])
    scale = 1.0 / (total_rows * column_count)
    spectra_pair = (
        lax.all_to_all(inverse_real, "xy", split_axis=2, concat_axis=3, tiled=True),
        lax.all_to_all(inverse_imag, "xy", split_axis=2, concat_axis=3, tiled=True),
    )
    widened = []
    for member in spectra_pair:
        filler = jnp.zeros(member.shape[:-1] + (column_count - 2 * KY,), jnp.float32)
        widened.append(jnp.concatenate([member[..., :KY], filler, member[..., KY:]], axis=3))
    plane_real, discarded = transform(widened[0], widened[1], 1.0, 0)
    planes = plane_real * scale
    tendency = (-planes[0] - vertical + wall_source[None] * inside).astype(jnp.bfloat16)
    return (tendency, planes[1])


def solution(mesh):
    return jax.shard_map(
        per_device,
        mesh=mesh,
        in_specs=(
            P("gz", "xy", None),
            P("gz", "xy", None),
            P("gz", "xy", None),
            P("gz", "xy", None),
            P("xy", None),
            P("xy", None),
            P(),
            P(),
        ),
        out_specs=(P("gz", "xy", None), P("gz", "xy", None)),
        check_vma=False,
    )
```

profile of v0, /device:TPU:0, one launch (start us, length us, event | category | flops | bytes accessed | tf_op | source)
XLA Modules:
  0.0 1030.2 jit_solution(14545386017519221230)
XLA Ops:
  43.5 10.5 %collective-permute-done = bf16[2,1,256,2048]{3,2,1,0:T(8,128)(2,1)} collective-permute-done((bf16[2,1,256,2048]{3,2,1,0:T(8,128)(2,1)}, bf16[2,1,256,2048]{3,2,1,0:T(8,128)(2,1)}, u32[]{:S(2)}, u32[]{:S(2)}) %collective-permute-start) | collective-permute-done | bytes 2097184 | tf_op jit(solution)/shard_map/ppermute | solution.py:41
  53.9 46.9 %collective-permute-done.1 = bf16[2,1,256,2048]{3,2,1,0:T(8,128)(2,1)} collective-permute-done((bf16[2,1,256,2048]{3,2,1,0:T(8,128)(2,1)}, bf16[2,1,256,2048]{3,2,1,0:T(8,128)(2,1)}, u32[]{:S(2)}, u32[]{:S(2)}) %collective-permute-start.1) | collective-permute-done | bytes 2097184 | tf_op jit(solution)/shard_map/ppermute | solution.py:42
  108.2 14.5 %fusion.6 = f32[32,5,256,64]{2,0,3,1:T(8,128)} fusion(f32[5,1,256,32,64]{2,3,4,0,1:T(8,128)} %copy_dynamic-update-slice_fusion), kind=kOutput, calls=%fused_computation.13 | convolution fusion | flops 1006647296 | bytes 20971520 | tf_op jit(solution)/shard_map/...ab,ac->...cb/dot_general | solution.py:66
  122.7 19.6 %fusion.1 = (f32[5,256,32,64]{1,2,3,0:T(8,128)}, f32[5,256,32,64]{1,2,3,0:T(8,128)}) fusion(f32[32,5,256,64]{2,0,3,1:T(8,128)} %fusion.6, f32[32,64]{0,1:T(8,128)S(1)} %get-tuple-element.98, f32[32,64]{0,1:T(8,128)S(1)} %get-tuple-element.99, f32[5,1,256,32,64]{2,3,4,0,1:T(8,128)} %copy_dynamic-update-slice_fusion), kind=kOutput, calls=%fused_computation.6 | convolution fusion | flops 1022375936 | bytes 41959424 | tf_op jit(solution)/shard_map/...ab,ac->...cb/dot_general | solution.py:66
  142.3 22.3 %fusion.8 = f32[5,256,32,64]{1,3,2,0:T(8,128)} fusion(f32[5,256,32,64]{1,2,3,0:T(8,128)} %get-tuple-element.32), kind=kOutput, calls=%fused_computation.17 | convolution fusion | flops 2013323264 | bytes 20971520 | tf_op jit(solution)/shard_map/...cb,bd->...cd/dot_general | solution.py:69
  164.6 16.6 %fusion.10 = f32[5,256,32,64]{1,3,2,0:T(8,128)} fusion(f32[5,256,32,64]{1,2,3,0:T(8,128)S(1)} %copy-done), kind=kOutput, calls=%fused_computation.19 | convolution fusion | flops 2013323264 | bytes 20971520 | tf_op jit(solution)/shard_map/...cb,bd->...cd/dot_general | solution.py:68
  181.2 22.6 %add_bitcast_fusion = f32[5,1,256,64,32]{2,3,4,0,1:T(8,128)} fusion(f32[5,256,32,64]{1,3,2,0:T(8,128)} %fusion.8, f32[5,256,32,64]{1,2,3,0:T(8,128)S(1)} %bitcast.333), kind=kOutput, calls=%fused_computation.15 | convolution fusion | flops 2015944704 | bytes 31457280 | tf_op jit(solution)/shard_map/...cb,bd->...cd/dot_general | solution.py:69
  218.6 23.0 %subtract_bitcast_fusion = f32[5,1,256,64,32]{2,3,4,0,1:T(8,128)} fusion(f32[5,256,32,64]{1,3,2,0:T(8,128)} %fusion.10, f32[5,256,32,64]{1,2,3,0:T(8,128)S(1)} %bitcast.333), kind=kOutput, calls=%fused_computation.16 | convolution fusion | flops 2015944704 | bytes 31457280 | tf_op jit(solution)/shard_map/...cb,bd->...cd/dot_general | solution.py:68
  274.9 10.3 %copy.339 = f32[4,1,256,1280]{2,1,0,3:T(1,128)} copy(f32[4,1,256,1280]{2,3,1,0:T(8,128)S(1)} %pad_maximum_fusion.1) | data formatting | bytes 10485760 | tf_op jit(solution)/shard_map/concatenate | solution.py:184
  293.4 10.3 %copy.330 = f32[4,1,256,1280]{2,1,0,3:T(1,128)} copy(f32[4,1,256,1280]{2,3,1,0:T(8,128)S(1)} %pad_maximum_fusion) | data formatting | bytes 10485760 | tf_op jit(solution)/shard_map/concatenate | solution.py:181
  303.7 103.1 %all-to-all-done.1 = f32[4,1,256,1280]{2,1,0,3:T(1,128)} async-done(((f32[4,1,256,1280]{2,1,0,3:T(1,128)}), f32[4,1,256,1280]{2,1,0,3:T(1,128)}, u32[]{:S(2)}, u32[]{:S(2)}) %all-to-all-start.1) | async-done | bytes 5242912 | tf_op jit(solution)/shard_map/all_to_all | solution.py:189
  431.7 12.7 %copy.342 = f32[4,32,64,160]{3,1,2,0:T(8,128)} copy(f32[4,32,64,160]{2,1,3,0:T(8,128)} %reshape.1375) | data formatting | bytes 10485760 | tf_op jit(solution)/shard_map/reshape.54
  444.4 11.8 %fusion.184 = f32[32,4,64,160]{3,0,2,1:T(8,128)} fusion(f32[4,32,64,160]{3,1,2,0:T(8,128)} %copy.342), kind=kOutput, calls=%fused_computation.289 | convolution fusion | flops 503330816 | bytes 10485760 | tf_op jit(solution)/shard_map/...abm,ac->...cbm/dot_general | solution.py:68
  466.0 61.9 %all-to-all-done = f32[4,1,256,1280]{2,1,0,3:T(1,128)} async-done(((f32[4,1,256,1280]{2,1,0,3:T(1,128)}), f32[4,1,256,1280]{2,1,0,3:T(1,128)}, u32[]{:S(2)}, u32[]{:S(2)}) %all-to-all-start) | async-done | bytes 5242912 | tf_op jit(solution)/shard_map/all_to_all | solution.py:188
  545.1 12.6 %copy.333 = f32[4,32,64,160]{3,1,2,0:T(8,128)} copy(f32[4,32,64,160]{2,1,3,0:T(8,128)} %reshape.1374) | data formatting | bytes 10485760 | tf_op jit(solution)/shard_map/reshape.42
  557.8 12.1 %fusion.182 = f32[32,4,64,160]{3,0,2,1:T(8,128)} fusion(f32[4,32,64,160]{3,1,2,0:T(8,128)} %copy.333), kind=kOutput, calls=%fused_computation.287 | convolution fusion | flops 503330816 | bytes 10485760 | tf_op jit(solution)/shard_map/...abm,ac->...cbm/dot_general | solution.py:69
  569.9 19.1 %fusion.17 = (f32[4,32,64,160]{3,1,2,0:T(8,128)}, f32[4,32,64,160]{3,1,2,0:T(8,128)}) fusion(f32[32,64]{0,1:T(8,128)S(1)} %copy-done.41, f32[32,64]{0,1:T(8,128)S(1)} %copy-done.43, f32[32,4,64,160]{3,0,2,1:T(8,128)} %fusion.182, f32[32,4,64,160]{3,0,2,1:T(8,128)} %fusion.187, f32[32,4,64,160]{3,0,2,1:T(8,128)} %fusion.184, f32[4,32,64,160]{3,1,2,0:T(8,128)} %copy.333), kind=kOutput, calls=%fused_computation.30 | convolution fusion | flops 513816576 | bytes 31473664 | tf_op jit(solution)/shard_map/...abm,ac->...cbm/dot_general | solution.py:68
  589.1 18.0 %fusion.22 = f32[64,4,32,160]{3,0,2,1:T(8,128)} fusion(f32[4,32,64,160]{3,1,2,0:T(8,128)} %get-tuple-element.30), kind=kOutput, calls=%fused_computation.39 | convolution fusion | flops 1006690304 | bytes 10485760 | tf_op jit(solution)/shard_map/...cbm,bd->...cdm/dot_general | solution.py:68
  607.1 12.6 %fusion.20 = f32[64,4,32,160]{3,0,2,1:T(8,128)S(1)} fusion(f32[4,32,64,160]{3,1,2,0:T(8,128)S(1)} %copy-done.2), kind=kOutput, calls=%fused_computation.37 | convolution fusion | flops 1006690304 | bytes 10485760 | tf_op jit(solution)/shard_map/...cbm,bd->...cdm/dot_general | solution.py:69
  619.8 15.7 %subtract_bitcast_fusion.1 = f32[4,1,64,32,160]{4,2,3,0,1:T(8,128)} fusion(f32[64,4,32,160]{3,0,2,1:T(8,128)} %fusion.22, f32[4,32,64,160]{3,1,2,0:T(8,128)S(1)} %bitcast.335), kind=kOutput, calls=%fused_computation.36 | convolution fusion | flops 1008001024 | bytes 15728640 | tf_op jit(solution)/shard_map/...cbm,bd->...cdm/dot_general | solution.py:68
  648.6 13.6 %add_bitcast_fusion.1 = f32[4,1,64,32,160]{4,2,3,0,1:T(8,128)} fusion(f32[64,4,32,160]{3,0,2,1:T(8,128)S(1)} %fusion.20, f32[4,32,64,160]{3,1,2,0:T(8,128)S(1)} %bitcast.335), kind=kOutput, calls=%fused_computation.35 | convolution fusion | flops 1008001024 | bytes 15728640 | tf_op jit(solution)/shard_map/...cbm,bd->...cdm/dot_general | solution.py:69
  750.9 10.7 %copy.377 = f32[2,1,2048,160]{3,1,0,2:T(1,128)} copy(f32[2,1,2048,160]{2,3,1,0:T(8,128)} %pad_maximum_fusion.5) | data formatting | bytes 5242880 | tf_op jit(solution)/shard_map/stack | solution.py:274
  794.9 65.7 %all-to-all-done.3 = f32[2,1,2048,160]{3,1,0,2:T(1,128)} async-done(((f32[2,1,2048,160]{3,1,0,2:T(1,128)}), f32[2,1,2048,160]{3,1,0,2:T(1,128)}, u32[]{:S(2)}, u32[]{:S(2)}) %all-to-all-start.3) | async-done | bytes 2621472 | tf_op jit(solution)/shard_map/all_to_all | solution.py:278
  877.9 81.6 %all-to-all-done.2 = f32[2,1,2048,160]{3,1,0,2:T(1,128)} async-done(((f32[2,1,2048,160]{3,1,0,2:T(1,128)}), f32[2,1,2048,160]{3,1,0,2:T(1,128)}, u32[]{:S(2)}, u32[]{:S(2)}) %all-to-all-start.2) | async-done | bytes 2621472 | tf_op jit(solution)/shard_map/all_to_all | solution.py:277
  (271 shorter events, 380.2 us)
Async XLA Ops:
  3.9 50.0 %collective-permute-start = (bf16[2,1,256,2048]{3,2,1,0:T(8,128)(2,1)}, bf16[2,1,256,2048]{3,2,1,0:T(8,128)(2,1)}, u32[]{:S(2)}, u32[]{:S(2)}) collective-permute-start(bf16[2,1,256,2048]{3,2,1,0:T(8,128)(2,1)} %pad_maximum_fusion.6), channel_id=1, source_target_pairs={{0,8},{8,16},{16,24},{1,9},{9,17},{17,25},{2,10},{10,18},{18,26},{... | collective-permute-start | bytes 6291464 | tf_op jit(solution)/shard_map/ppermute | solution.py:41
  10.1 90.8 %collective-permute-start.1 = (bf16[2,1,256,2048]{3,2,1,0:T(8,128)(2,1)}, bf16[2,1,256,2048]{3,2,1,0:T(8,128)(2,1)}, u32[]{:S(2)}, u32[]{:S(2)}) collective-permute-start(bf16[2,1,256,2048]{3,2,1,0:T(8,128)(2,1)} %pad_maximum_fusion.6), channel_id=1, source_target_pairs={{8,0},{16,8},{24,16},{9,1},{17,9},{25,17},{10,2},{18,10},{26,18},{... | collective-permute-start | bytes 6291464 | tf_op jit(solution)/shard_map/ppermute | solution.py:42
  33.0 378.4 %copy-start.46 = (f32[2048]{0:T(1024)}, f32[2048]{0:T(1024)S(1)}, u32[]{:S(2)}) copy-start(f32[2048]{0:T(1024)S(1)} %convert_multiply_fusion.5) | copy-start | bytes 24580
  33.2 89.5 %copy-start.40 = (f32[32,64]{0,1:T(8,128)}, f32[32,64]{0,1:T(8,128)S(1)}, u32[]{:S(2)}) copy-start(f32[32,64]{0,1:T(8,128)S(1)} %get-tuple-element.98) | copy-start | bytes 24580
  33.2 89.5 %copy-start.42 = (f32[32,64]{0,1:T(8,128)}, f32[32,64]{0,1:T(8,128)S(1)}, u32[]{:S(2)}) copy-start(f32[32,64]{0,1:T(8,128)S(1)} %get-tuple-element.99) | copy-start | bytes 24580
  40.9 59.9 %copy-start.6 = (bf16[1,256,2048]{2,1,0:T(8,128)(2,1)S(1)}, bf16[1,256,2048]{2,1,0:T(8,128)(2,1)}, u32[]{:S(2)}) copy-start(bf16[1,256,2048]{2,1,0:T(8,128)(2,1)} %param.10) | copy-start | bytes 3145732
  142.3 22.3 %copy-start = (f32[5,256,32,64]{1,2,3,0:T(8,128)S(1)}, f32[5,256,32,64]{1,2,3,0:T(8,128)}, u32[]{:S(2)}) copy-start(f32[5,256,32,64]{1,2,3,0:T(8,128)} %get-tuple-element.32) | copy-start | bytes 31457284
  142.3 38.9 %slice-start = ((s8[10485760]{0:T(1024)(128)(4,1)}), s8[4194304]{0:T(1024)(128)(4,1)S(1)}, s32[]{:S(2)}) async-start(s8[10485760]{0:T(1024)(128)(4,1)} %bitcast.332), calls=%async_computation.4 | async-start | bytes 8388608
  142.3 38.9 %slice-start.1 = ((s8[10485760]{0:T(1024)(128)(4,1)}), s8[4194304]{0:T(1024)(128)(4,1)S(1)}, s32[]{:S(2)}) async-start(s8[10485760]{0:T(1024)(128)(4,1)} %bitcast.332), calls=%async_computation.5 | async-start | bytes 8388608
  164.6 16.6 %slice-start.2 = ((s8[10485760]{0:T(1024)(128)(4,1)}), s8[2097152]{0:T(1024)(128)(4,1)S(1)}, s32[]{:S(2)}) async-start(s8[10485760]{0:T(1024)(128)(4,1)} %bitcast.332), calls=%async_computation.6 | async-start | bytes 4194304
  285.2 121.5 %all-to-all-start.1 = ((f32[4,1,256,1280]{2,1,0,3:T(1,128)}), f32[4,1,256,1280]{2,1,0,3:T(1,128)}, u32[]{:S(2)}, u32[]{:S(2)}) async-start(f32[4,1,256,1280]{2,1,0,3:T(1,128)} %copy.339), calls=%async_computation.1 | async-start | bytes 10485760 | tf_op jit(solution)/shard_map/all_to_all | solution.py:189
  406.7 121.2 %all-to-all-start = ((f32[4,1,256,1280]{2,1,0,3:T(1,128)}), f32[4,1,256,1280]{2,1,0,3:T(1,128)}, u32[]{:S(2)}, u32[]{:S(2)}) async-start(f32[4,1,256,1280]{2,1,0,3:T(1,128)} %copy.330), calls=%async_computation | async-start | bytes 10485760 | tf_op jit(solution)/shard_map/all_to_all | solution.py:188
  589.1 18.0 %copy-start.2 = (f32[4,32,64,160]{3,1,2,0:T(8,128)S(1)}, f32[4,32,64,160]{3,1,2,0:T(8,128)}, u32[]{:S(2)}) copy-start(f32[4,32,64,160]{3,1,2,0:T(8,128)} %get-tuple-element.30) | copy-start | bytes 15728644
  589.1 30.7 %slice-start.3 = ((s8[8388608]{0:T(1024)(128)(4,1)}), s8[4194304]{0:T(1024)(128)(4,1)S(1)}, s32[]{:S(2)}) async-start(s8[8388608]{0:T(1024)(128)(4,1)} %bitcast.334), calls=%async_computation.7 | async-start | bytes 8388608
  692.5 9.0 collective-permute-start.2
  701.6 5.5 collective-permute-start.3
  707.2 6.5 collective-permute-start.4
  713.9 13.5 %copy-start.33 = (f32[1,128,160]{1,2,0:T(8,128)}, f32[1,128,160]{1,2,0:T(8,128)S(1)}, u32[]{:S(2)}) copy-start(f32[1,128,160]{1,2,0:T(8,128)S(1)} %get-tuple-element.16) | copy-start | bytes 245764
  714.0 13.5 %copy-start.30 = (f32[1,128,160]{1,2,0:T(8,128)}, f32[1,128,160]{1,2,0:T(8,128)S(1)}, u32[]{:S(2)}) copy-start(f32[1,128,160]{1,2,0:T(8,128)S(1)} %get-tuple-element.18) | copy-start | bytes 245764
  714.0 6.3 collective-permute-start.5
  720.4 7.0 collective-permute-start.6
  728.2 9.0 collective-permute-start.7
  761.6 99.0 %all-to-all-start.3 = ((f32[2,1,2048,160]{3,1,0,2:T(1,128)}), f32[2,1,2048,160]{3,1,0,2:T(1,128)}, u32[]{:S(2)}, u32[]{:S(2)}) async-start(f32[2,1,2048,160]{3,1,0,2:T(1,128)} %copy.377), calls=%async_computation.3 | async-start | bytes 8388608 | tf_op jit(solution)/shard_map/all_to_all | solution.py:278
  860.6 99.0 %all-to-all-start.2 = ((f32[2,1,2048,160]{3,1,0,2:T(1,128)}), f32[2,1,2048,160]{3,1,0,2:T(1,128)}, u32[]{:S(2)}, u32[]{:S(2)}) async-start(f32[2,1,2048,160]{3,1,0,2:T(1,128)} %copy.369), calls=%async_computation.2 | async-start | bytes 8388608 | tf_op jit(solution)/shard_map/all_to_all | solution.py:277
  (46 other events, 253.7 us)
where the time goes:
time: 1040 us; the launch traced here: 1030 us
  waiting for transfers between devices  373 us (36%)
  matrix products  319 us (31%)
  local copies, waits for them, and re-layouts  249 us (24%)
  other arithmetic  44.5 us (4%)
  starting transfers between devices  41.7 us (4%)
    all_to_all x1, waiting for transfers between devices, per_device(): lax.all_to_all(narrow_imag, 'xy', split_axis=3, concat_axis=2, tiled=True)  103 us
    dot_general x8, matrix products, contract(): multiply(real_part, cosines) - multiply(imag_part, sines)  82.6 us
    all_to_all x1, waiting for transfers between devices, per_device(): lax.all_to_all(inverse_real, 'xy', split_axis=2, concat_axis=3, tiled=True)  81.6 us
    dot_general x8, matrix products, contract(): multiply(imag_part, sines)  71.9 us
    dot_general x7, matrix products, contract(): multiply(real_part, sines) + multiply(imag_part, cosines)  68.8 us
    all_to_all x1, waiting for transfers between devices, per_device(): lax.all_to_all(inverse_imag, 'xy', split_axis=2, concat_axis=3, tiled=True)  65.7 us
    dot_general x7, matrix products, contract(): multiply(imag_part, cosines)  62.1 us
    all_to_all x1, waiting for transfers between devices, per_device(): lax.all_to_all(narrow_real, 'xy', split_axis=3, concat_axis=2, tiled=True)  61.9 us
  transfers between devices with their start and end apart: 12, of which 8 were waited for; matrix products, arithmetic and copies ran while one was open for 16% of the time, Pallas kernels for 0%

commit v1 on v0

v1 whole, which is shorter than its diff:
```python
from functools import partial
import math

import jax
import jax.numpy as jnp
import ml_dtypes
import numpy as np
from jax import lax
from jax.sharding import PartitionSpec as P

KX = 640
KY = 640
BAND = 64

GRID_STEP = 2.5
LEVEL_STEP = 2.5
DRAG_STEP = 0.5
GUST_FLOOR = 0.25

BF = jnp.bfloat16
F32 = jnp.float32


def round_up(value, unit):
    return -(-value // unit) * unit


def split_np(table):
    high = table.astype(ml_dtypes.bfloat16)
    low = (table - high.astype(np.float64)).astype(ml_dtypes.bfloat16)
    return high, low


def split(array):
    high = lax.reduce_precision(array, exponent_bits=8, mantissa_bits=7)
    return high.astype(BF), (array - high).astype(BF)


def mode_rows(modes_c, modes_s, count):
    t = np.arange(count)
    cos_rows = np.cos(2.0 * np.pi / count * (np.outer(modes_c, t) % count))
    sin_rows = np.sin(2.0 * np.pi / count * (np.outer(modes_s, t) % count))
    return cos_rows, sin_rows


def y_layout(strips, count):
    half = KY // strips
    share = round_up(2 * half + 2, 8)
    table = np.zeros((strips, share, count))
    synth = np.zeros((strips, share))
    wave = np.zeros((strips, share))
    for d in range(strips):
        modes = np.arange(d * half, (d + 1) * half)
        table[d, :half], table[d, half : 2 * half] = mode_rows(modes, modes, count)
        wave[d, :half] = wave[d, half : 2 * half] = modes
        synth[d, : 2 * half] = 2.0 / count
    synth[0, 0] = 1.0 / count
    ends = np.array([KY])
    cos_end, sin_end = mode_rows(ends, ends, count)
    table[-1, 2 * half], table[-1, 2 * half + 1] = cos_end[0], sin_end[0]
    wave[-1, 2 * half : 2 * half + 2] = KY
    synth[-1, 2 * half : 2 * half + 2] = 1.0 / count
    wave *= 2.0 * np.pi / (count * GRID_STEP)
    return half, share, table.reshape(strips * share, count), wave, synth


def x_band(count):
    width = round_up(2 * BAND + 2, 8)
    modes = np.arange(BAND)
    basis = np.zeros((width, count))
    basis[:BAND], basis[BAND : 2 * BAND] = mode_rows(modes, modes, count)
    ends = np.array([BAND])
    cos_end, sin_end = mode_rows(ends, ends, count)
    basis[2 * BAND], basis[2 * BAND + 1] = cos_end[0], sin_end[0]
    unit = 2.0 * np.pi / (count * GRID_STEP)
    wave = np.zeros(width)
    wave[:BAND] = wave[BAND : 2 * BAND] = modes * unit
    wave[2 * BAND : 2 * BAND + 2] = BAND * unit
    slope = np.zeros((width, count))
    slope[:BAND] = wave[:BAND, None] * basis[BAND : 2 * BAND]
    slope[BAND : 2 * BAND] = -wave[:BAND, None] * basis[:BAND]
    slope[2 * BAND] = wave[2 * BAND] * basis[2 * BAND + 1]
    slope[2 * BAND + 1] = -wave[2 * BAND] * basis[2 * BAND]
    synth = np.zeros(width)
    synth[: 2 * BAND] = 2.0 / count
    synth[0] = 1.0 / count
    synth[2 * BAND : 2 * BAND + 2] = 1.0 / count
    return width, basis, slope, wave, synth


def x_operators(count):
    modes = np.arange(1, KX)
    unit = 2.0 * np.pi / (count * GRID_STEP)
    lag = np.arange(count)
    angle = 2.0 * np.pi / count * (np.outer(modes, lag) % count)
    end_angle = 2.0 * np.pi / count * (KX * lag % count)
    slope = -(2.0 * (modes * unit) @ np.sin(angle) + KX * unit * np.sin(end_angle)) / count
    keep = (1.0 + 2.0 * np.cos(angle).sum(axis=0) + np.cos(end_angle)) / count
    shift = (lag[None, :] - lag[:, None]) % count
    ends = 2.0 * np.pi / count * (KX * lag % count)
    return slope[shift], keep[shift], np.cos(ends), np.sin(ends), KX * unit


def swap_scaled(array, half, wave):
    cos_part = array[..., :half, :]
    sin_part = array[..., half : 2 * half, :]
    cos_end = array[..., 2 * half : 2 * half + 1, :]
    sin_end = array[..., 2 * half + 1 : 2 * half + 2, :]
    rest = array[..., 2 * half + 2 :, :]
    swapped = jnp.concatenate([sin_part, -cos_part, sin_end, -cos_end, rest], axis=-2)
    return swapped * wave


def dot(a, b, dims):
    return lax.dot_general(a, b, (dims, ((), ())), preferred_element_type=F32)


def per_device(tables, u_wind, v_wind, w_wind, scalar, heights, wall_class, wall_area, wall_heat):
    _, row_count, column_count = u_wind.shape
    strips = lax.axis_size("xy")
    groups = lax.axis_size("gz")
    level = lax.axis_index("gz")
    strip = lax.axis_index("xy")
    half, share, width = tables["half"], tables["share"], tables["width"]
    count_x = row_count * strips

    w_flat, c_flat = w_wind[0], scalar[0]
    up = [(i, i + 1) for i in range(groups - 1)]
    down = [(i + 1, i) for i in range(groups - 1)]
    c_below = lax.ppermute(c_flat, "gz", up)

    inside = level < heights
    density = jnp.zeros(heights.shape, F32)
    heat = jnp.zeros(heights.shape, F32)
    for k in range(wall_area.shape[0]):
        match = wall_class == k
        density = jnp.where(match, wall_area[k], density)
        heat = jnp.where(match, wall_heat[k], heat)
    east, north = u_wind[0].astype(F32), v_wind[0].astype(F32)
    tracer = c_flat.astype(F32)
    speed = jnp.sqrt(east * east + north * north + GUST_FLOOR)
    drag = 1.0 + jnp.where(inside, DRAG_STEP * density * speed, 0.0)
    east_star = east / drag
    north_star = north / drag
    heating = jnp.where(inside, heat, 0.0)

    first_row = strip * row_count
    rows = lambda t: lax.dynamic_slice_in_dim(t, first_row, row_count, 1)
    basis = jnp.concatenate([rows(tables["basis"][0]), rows(tables["basis"][1])], axis=1)
    slope = jnp.concatenate([rows(tables["slope"][0]), rows(tables["slope"][1])], axis=1)
    mn = ((1,), (0,))

    def low_modes(table, field):
        high, low = split(field)
        return dot(table, jnp.concatenate([high, high], axis=0), mn) + dot(
            table[:, :row_count], low, mn
        )

    w_modes = dot(basis, jnp.concatenate([w_flat, w_flat], axis=0), mn) * (1.0 / LEVEL_STEP)
    a_modes = low_modes(slope, east_star) - w_modes
    b_modes = low_modes(basis, north_star)
    modes_high, modes_low = split(jnp.concatenate([a_modes, w_modes, b_modes], axis=0))
    fields = jnp.concatenate(
        [
            (east_star * tracer).astype(BF),
            (north_star * tracer).astype(BF),
            modes_high,
            modes_low,
        ],
        axis=0,
    )
    y_high, y_low = tables["y"]
    nt = ((1,), (1,))
    spectra = dot(y_high, fields, nt)
    low = dot(y_low, modes_high, nt)
    spectra = spectra.reshape(strips, share, -1)
    low = low.reshape(strips, share, -1)
    first = 2 * row_count
    press = spectra[..., first : first + 3 * width] + spectra[..., first + 3 * width :] + low
    wave_y = jnp.asarray(tables["wave_y"], F32)[..., None]
    flux_v = swap_scaled(spectra[..., row_count : 2 * row_count], half, wave_y)
    rhs_part = press[..., :width] + swap_scaled(press[..., 2 * width :], half, wave_y)
    sent = jnp.concatenate(
        [spectra[..., :row_count], flux_v, rhs_part, press[..., width : 2 * width]], axis=-1
    ).astype(BF)
    got = lax.all_to_all(sent, "xy", split_axis=0, concat_axis=0, tiled=True)

    flux = w_flat.astype(F32) * (tracer + c_below.astype(F32)) * (0.5 / LEVEL_STEP)
    flux_above = lax.ppermute(flux.astype(BF), "gz", down)

    sums = jnp.sum(got[..., 2 * row_count :].astype(F32), axis=0)
    all_sums = lax.all_gather(sums, "gz", axis=0, tiled=False)
    wave_own = lax.dynamic_index_in_dim(
        jnp.asarray(tables["wave_y"], F32), strip, 0, keepdims=False
    )
    wave_x = jnp.asarray(tables["wave_x"], F32)
    coupling = 1.0 / (LEVEL_STEP * LEVEL_STEP)
    diagonal = -2.0 * coupling - (wave_x * wave_x)[None, :] - (wave_own * wave_own)[:, None]
    ratio = jnp.zeros_like(diagonal)
    reduced = jnp.zeros_like(diagonal)
    ratios, reduced_list = [], []
    for l in range(groups):
        rhs = all_sums[l, :, :width]
        if l + 1 < groups:
            rhs = rhs + all_sums[l + 1, :, width:]
        inverse = 1.0 / (diagonal - coupling * ratio)
        ratio = coupling * inverse
        reduced = (rhs - coupling * reduced) * inverse
        ratios.append(ratio)
        reduced_list.append(reduced)
    value = jnp.zeros_like(diagonal)
    own = jnp.zeros_like(diagonal)
    for l in reversed(range(groups)):
        value = reduced_list[l] - ratios[l] * value
        own = jnp.where(level == l, value, own)
    corner = own[2 * half : 2 * half + 2, 2 * BAND : 2 * BAND + 2]
    sign = np.array([[-1.0, 1.0], [1.0, -1.0]], np.float32)
    fixed = corner + sign * corner[::-1, ::-1]
    corner = jnp.where(strip == strips - 1, fixed, corner)
    own = lax.dynamic_update_slice(own, corner, (2 * half, 2 * BAND))
    synth_y = lax.dynamic_index_in_dim(
        jnp.asarray(tables["synth_y"], F32), strip, 0, keepdims=False
    )[:, None]
    own = own * (synth_y * jnp.asarray(tables["synth_x"], F32)[None, :] * tables["gain"])

    z_east = jnp.swapaxes(got[..., :row_count], 0, 1).reshape(share, count_x)
    z_north = jnp.swapaxes(got[..., row_count : 2 * row_count], 0, 1).reshape(share, count_x)
    both = jnp.concatenate([z_east, z_north], axis=1)
    product = dot(both, tables["x_high"], mn)
    if tables["x_low"] is not None:
        product = product + dot(both, tables["x_low"], mn)
    ends = jnp.asarray(tables["ends"], F32)
    pair = both[2 * half : 2 * half + 2].astype(F32)
    pe, pn = pair[:, :count_x], pair[:, count_x:]
    top = tables["top"]
    ec, es = jnp.sum(pe * ends[0], axis=1), jnp.sum(pe * ends[1], axis=1)
    nc, ns = jnp.sum(pn * ends[0], axis=1), jnp.sum(pn * ends[1], axis=1)
    cos_gain = (-top * ec + ns) / count_x
    sin_gain = (-top * es - nc) / count_x
    imag = cos_gain[:, None] * ends[0] + sin_gain[:, None] * ends[1]
    imag = jnp.where(strip == strips - 1, jnp.stack([-imag[1], imag[0]]), 0.0)
    product = lax.dynamic_update_slice(
        product, product[2 * half : 2 * half + 2] + imag, (2 * half, 0)
    )
    product = product * synth_y
    back = jnp.swapaxes(product.reshape(share, strips, row_count), 0, 1).astype(BF)
    own = jnp.broadcast_to(own.astype(BF)[None], (strips, share, width))
    returned = lax.all_to_all(
        jnp.concatenate([back, own], axis=-1), "xy", split_axis=0, concat_axis=0, tiled=True
    ).reshape(strips * share, row_count + width)

    tn = ((0,), (0,))
    planes = dot(returned, y_high, tn)
    if tables["low_back"]:
        planes = planes + dot(returned, y_low, tn)
        pressed = planes[row_count:]
    else:
        pressed = planes[row_count:] + dot(returned[:, row_count:], y_low, tn)
    p_high, p_low = split(pressed)
    b_high, b_low = rows(tables["basis"][0]), rows(tables["basis"][1])
    pressure = dot(
        jnp.concatenate([b_high, b_low, b_high], axis=0),
        jnp.concatenate([p_high, p_high, p_low], axis=0),
        tn,
    ) * (1.0 / tables["gain"])
    vertical = flux_above.astype(F32) - flux
    tendency = (heating - planes[:row_count] - vertical).astype(BF)
    return (tendency[None], pressure[None])


OPTIONS = {"low_back": False, "x_low": False}


def solution(mesh):

    def whole(u_wind, *others):
        _, count_x, count_y = u_wind.shape
        strips = mesh.shape["xy"]
        half, share, y_table, wave_y, synth_y = y_layout(strips, count_y)
        width, basis, slope, wave_x, synth_x = x_band(count_x)
        x_slope, x_keep, end_cos, end_sin, top = x_operators(count_x)
        x_high, x_low = split_np(np.concatenate([x_slope, x_keep], axis=0))
        tables = {
            "half": half,
            "share": share,
            "width": width,
            "y": split_np(y_table),
            "wave_y": wave_y,
            "synth_y": synth_y,
            "basis": split_np(basis),
            "slope": split_np(slope),
            "wave_x": wave_x,
            "synth_x": synth_x,
            "gain": float(count_x),
            "x_high": x_high,
            "x_low": x_low if OPTIONS["x_low"] else None,
            "ends": np.stack([end_cos, end_sin]),
            "top": top,
            "low_back": OPTIONS["low_back"],
        }
        return jax.shard_map(
            partial(per_device, tables),
            mesh=mesh,
            in_specs=(P("gz", "xy", None),) * 4 + (P("xy", None),) * 2 + (P(), P()),
            out_specs=(P("gz", "xy", None), P("gz", "xy", None)),
            check_vma=False,
        )(u_wind, *others)

    return whole
```

time: 1040 us -> 243 us (0.23)
  matrix products: 319 us -> 36.3 us
  waiting for transfers between devices: 373 us -> 103 us
  local copies, waits for them, and re-layouts: 249 us -> 24.6 us
  starting transfers between devices: 41.7 us -> 14.8 us
  blocking collectives: 0 us -> 15 us
    dot_general x32 -> x12, matrix products: 319 us -> 36.3 us  [dot(): return lax.dot_general(a, b, (dims, ((), ())), preferred_element_type=F32)]
    all_to_all x4 -> x2, waiting for transfers between devices: 312 us -> 86.6 us  [the longest x1 55 us: per_device(): got = lax.all_to_all(sent, 'xy', split_axis=0, concat_axis=0, tiled=True)]
    slice x30 -> x7, local copies, waits for them, and re-layouts: 80 us -> 4.45 us  [the longest x1 1.63 us: per_device(): density = jnp.where(match, wall_area[k], density)]
    another operation x10 -> x0, local copies, waits for them, and re-layouts: 66.3 us -> none
    ppermute x8 -> x2, waiting for transfers between devices: 61.3 us -> 16.9 us  [the longest x1 16.9 us: per_device(): c_below = lax.ppermute(c_flat, 'gz', up)]
    all_to_all x8 -> x0, local copies, waits for them, and re-layouts: 36.7 us -> none  [the longest x2 9.54 us: per_device(): lax.all_to_all(inverse_imag, 'xy', split_axis=2, concat_axis=3, tiled=True)]
    unnamed x123 -> x83, local copies, waits for them, and re-layouts: 19.5 us -> 2.28 us
    convert_element_type x7 -> x8, other arithmetic: 5.51 us -> 22.6 us  [the longest x1 12.2 us: per_device(): (east_star * tracer).astype(BF)]
  transfers between devices with their start and end apart: 12 -> 4, of which waited for: 8 -> 3; matrix products, arithmetic and copies ran while one was open for 16% -> 6% of each run, Pallas kernels for 0% -> 0%
where the time goes in v1:
time: 243 us; the launch traced here: 242 us
  waiting for transfers between devices  103 us (42%)
  other arithmetic  46.2 us (19%)
  matrix products  36.3 us (15%)
  local copies, waits for them, and re-layouts  24.6 us (10%)
  blocking collectives  15 us (6%)
  starting transfers between devices  14.8 us (6%)
    all_to_all x1, waiting for transfers between devices, per_device(): got = lax.all_to_all(sent, 'xy', split_axis=0, concat_axis=0, tiled=True)  55 us
    dot_general x12, matrix products, dot(): return lax.dot_general(a, b, (dims, ((), ())), preferred_element_type=F32)  36.3 us
    all_to_all x1, waiting for transfers between devices, per_device(): lax.all_to_all(jnp.concatenate([back, own], axis=-1), 'xy', split_axis=0,...  31.6 us
    ppermute x1, waiting for transfers between devices, per_device(): c_below = lax.ppermute(c_flat, 'gz', up)  16.9 us
    all_gather x1, blocking collectives, per_device(): all_sums = lax.all_gather(sums, 'gz', axis=0, tiled=False)  15 us
    concatenate x2, local copies, waits for them, and re-layouts, swap_scaled(): jnp.concatenate([sin_part, -cos_part, sin_end, -cos_end, rest], axis=-2)  13.8 us
    convert_element_type x1, other arithmetic, per_device(): (east_star * tracer).astype(BF)  12.2 us
    broadcast_in_dim x1, other arithmetic, per_device(): return (tendency[None], pressure[None])  10 us
  transfers between devices with their start and end apart: 4, of which 3 were waited for; matrix products, arithmetic and copies ran while one was open for 6% of the time, Pallas kernels for 0%

profile of v1, /device:TPU:0, one launch (start us, length us, event | category | flops | bytes accessed | tf_op | source)
XLA Modules:
  0.0 241.8 jit_solution(3914076541166949015)
XLA Ops:
  0.6 4.9 %collective-permute-start = (bf16[256,2048]{1,0:T(8,128)(2,1)}, bf16[256,2048]{1,0:T(8,128)(2,1)S(1)}, u32[]{:S(2)}, u32[]{:S(2)}) collective-permute-start(bf16[256,2048]{1,0:T(8,128)(2,1)} %bitcast.113), channel_id=1, source_target_pairs={{0,8},{8,16},{16,24},{1,9},{9,17},{17,25},{2,10},{10,18},{18,26},{... | collective-permute-start | bytes 3145736 | tf_op jit(solution)/shard_map/ppermute | solution.py:130
  5.6 1.6 fusion.84
  9.1 2.2 convolution_multiply_fusion.1
  11.3 16.9 %collective-permute-done = bf16[256,2048]{1,0:T(8,128)(2,1)S(1)} collective-permute-done((bf16[256,2048]{1,0:T(8,128)(2,1)}, bf16[256,2048]{1,0:T(8,128)(2,1)S(1)}, u32[]{:S(2)}, u32[]{:S(2)}) %collective-permute-start) | collective-permute-done | bytes 1048608 | tf_op jit(solution)/shard_map/ppermute | solution.py:130
  28.2 12.2 %fusion.20 = (bf16[256,2048]{1,0:T(8,128)(2,1)}, f32[256,2048]{1,0:T(8,128)S(1)}, pred[256,2048]{1,0:T(8,128)(4,1)S(1)}, pred[256,2048]{1,0:T(8,128)(4,1)S(1)}, ...) fusion(bf16[1,256,2048]{2,1,0:T(8,128)(2,1)S(1)} %copy-done, ...), kind=kLoop, calls=%fused_computation.42 | loop fusion | flops 19398656 | bytes 18350116 | tf_op jit(solution)/shard_map/convert_element_type | solution.py:165
  40.6 9.3 %fusion.21 = (bf16[256,2048]{1,0:T(8,128)(2,1)}, f32[256,2048]{1,0:T(8,128)S(1)}) fusion(bf16[1,256,2048]{2,1,0:T(8,128)(2,1)S(1)} %copy-done, pred[256,2048]{1,0:T(8,128)(4,1)S(1)} %get-tuple-element.18, bf16[1,256,2048]{2,1,0:T(8,128)(2,1)S(1)} %copy-done.19, pred[256,2048]{1,0:T(8,128)(4,1)S(1)} %get-tuple-element.17, ...), kind=kLoop, calls=%fused_computation.43 | loop fusion | flops 11534336 | bytes 11010080 | tf_op jit(solution)/shard_map/convert_element_type | solution.py:166
  54.3 12.6 %fusion = f32[1344,1328]{1,0:T(8,128)S(1)} fusion(bf16[1344,2048]{1,0:T(8,128)(2,1)} %constant.107.clone, bf16[408,2048]{1,0:T(8,128)(2,1)S(1)} %get-tuple-element.25, bf16[408,2048]{1,0:T(8,128)(2,1)S(1)} %get-tuple-element.26, bf16[256,2048]{1,0:T(8,128)(2,1)} %get-tuple-element.19, bf16[256,2048]{1,0:T(8,128)(2,1)} %get-tuple-element.8), kind=kOutput, calls=%fused_computation | convolution fusion | flops 7332429824 | bytes 18083840 | tf_op jit(solution)/shard_map/dot_general | solution.py:115
  68.8 3.1 %fusion.85 = f32[1344,408]{1,0:T(8,128)S(1)} fusion(bf16[1344,2048]{1,0:T(8,128)(2,1)S(1)} %bitcast.124, bf16[408,2048]{1,0:T(8,128)(2,1)S(1)} %get-tuple-element.26), kind=kOutput, calls=%fused_computation.160 | convolution fusion | flops 2246049792 | bytes 9369600 | tf_op jit(solution)/shard_map/dot_general | solution.py:115
  72.8 1.5 slice_negate_fusion
  77.2 6.9 %concatenate.50 = f32[8,168,256]{2,1,0:T(8,128)} concatenate(f32[8,80,256]{2,1,0:T(8,128)} %get-tuple-element.24, f32[8,80,256]{2,1,0:T(8,128)} %get-tuple-element.23, f32[8,1,256]{2,1,0:T(1,128)} %get-tuple-element.22, f32[8,1,256]{2,1,0:T(1,128)} %get-tuple-element.21, f32[8,6,256]{2,1,0:T(8,128)S(1)} %slice.237), dimensions={1} | concatenate | bytes 2752512 | tf_op jit(solution)/shard_map/concatenate | solution.py:110
  84.1 2.5 %multiply_convert_fusion.1 = bf16[8,168,256]{2,1,0:T(8,128)(2,1)} fusion(f32[8,168,256]{2,1,0:T(8,128)} %concatenate.50, f32[8,168]{1,0:T(8,128)S(1)} %copy-done.28), kind=kLoop, calls=%fused_computation.74 | loop fusion | flops 688128 | bytes 2069760 | tf_op jit(solution)/shard_map/convert.3 | solution.py:301
  86.6 6.9 %concatenate.51 = f32[8,168,136]{2,1,0:T(8,128)} concatenate(f32[8,80,136]{2,1,0:T(8,128)} %get-tuple-element.30, f32[8,80,136]{2,1,0:T(8,128)} %get-tuple-element.29, f32[8,1,136]{2,1,0:T(1,128)} %get-tuple-element.28, f32[8,1,136]{2,1,0:T(1,128)} %get-tuple-element.27, f32[8,6,136]{2,1,0:T(8,128)S(1)} %slice.245), dimensions={1} | concatenate | bytes 1462272 | tf_op jit(solution)/shard_map/concatenate | solution.py:110
  93.6 1.7 fusion.42
  95.5 2.2 pad_maximum_fusion.1
  97.7 4.9 %all-to-all-start = ((bf16[8,168,784]{2,1,0:T(8,128)(2,1)}), bf16[8,168,784]{2,1,0:T(8,128)(2,1)S(1)}, u32[]{:S(2)}, u32[]{:S(2)}) async-start(bf16[8,168,784]{2,1,0:T(8,128)(2,1)} %pad_maximum_fusion.1), calls=%async_computation | async-start | bytes 4816896 | tf_op jit(solution)/shard_map/all_to_all | solution.py:186
  103.3 55.0 %all-to-all-done = bf16[8,168,784]{2,1,0:T(8,128)(2,1)S(1)} async-done(((bf16[8,168,784]{2,1,0:T(8,128)(2,1)}), bf16[8,168,784]{2,1,0:T(8,128)(2,1)S(1)}, u32[]{:S(2)}, u32[]{:S(2)}) %all-to-all-start) | async-done | bytes 2107424 | tf_op jit(solution)/shard_map/all_to_all | solution.py:186
  159.4 5.4 %fusion.86 = f32[168,2048]{1,0:T(8,128)S(1)} fusion(bf16[168,2048]{1,0:T(8,128)(2,1)S(1)} %bitcast.115, bf16[2048,2048]{1,0:T(8,128)(2,1)} %constant.120), kind=kOutput, calls=%fused_computation.161 | convolution fusion | flops 1409286144 | bytes 10452992 | tf_op jit(solution)/shard_map/dot_general | solution.py:115
  164.8 1.7 convolution_add_fusion.2
  167.8 15.0 %all-gather = f32[672,272]{1,0:T(8,128)S(1)} all-gather(f32[168,272]{1,0:T(8,128)S(1)} %convert_reduce_fusion), channel_id=2, replica_groups=mesh['gz'=4,'xy'=8] {'gz'}, dimensions={0}, use_global_device_ids=true | all-gather | bytes 913920 | tf_op jit(solution)/shard_map/all_gather | solution.py:192
  185.0 3.7 %all-to-all-start.1 = ((bf16[8,168,392]{2,1,0:T(8,128)(2,1)}), bf16[8,168,392]{2,1,0:T(8,128)(2,1)S(1)}, u32[]{:S(2)}, u32[]{:S(2)}) async-start(bf16[8,168,392]{2,1,0:T(8,128)(2,1)} %pad_maximum_fusion.2), calls=%async_computation.1 | async-start | bytes 2752512 | tf_op jit(solution)/shard_map/all_to_all | solution.py:248
  190.7 31.6 %all-to-all-done.1 = bf16[8,168,392]{2,1,0:T(8,128)(2,1)S(1)} async-done(((bf16[8,168,392]{2,1,0:T(8,128)(2,1)}), bf16[8,168,392]{2,1,0:T(8,128)(2,1)S(1)}, u32[]{:S(2)}, u32[]{:S(2)}) %all-to-all-start.1) | async-done | bytes 1053728 | tf_op jit(solution)/shard_map/all_to_all | solution.py:248
  222.3 4.8 %fusion.87 = f32[392,2048]{1,0:T(8,128)S(1)} fusion(bf16[1344,392]{1,0:T(8,128)(2,1)S(1)} %bitcast.129, bf16[1344,2048]{1,0:T(8,128)(2,1)} %constant.107.clone), kind=kOutput, calls=%fused_computation.162 | convolution fusion | flops 2157969408 | bytes 9769984 | tf_op jit(solution)/shard_map/dot_general | solution.py:115
  228.3 2.1 fusion.10
  231.8 10.0 %fusion.47 = bf16[1,256,2048]{2,1,0:T(8,128)(2,1)} fusion(bf16[256,2048]{1,0:T(8,128)(2,1)S(1)} %copy-done.23, bf16[256,2048]{1,0:T(8,128)(2,1)} %collective-permute-done.1, f32[392,2048]{1,0:T(8,128)S(1)} %fusion.87, pred[256,2048]{1,0:T(8,128)(4,1)S(1)} %copy-done.17, pred[256,2048]{1,0:T(8,128)(4,1)S(1)} %copy-done.15, ...), kind=kLoop, calls=%fused_computation.86 | loop fusion | flops 10485760 | bytes 12058656 | tf_op jit(solution)/shard_map/broadcast_in_dim | solution.py:268
  (129 shorter events, 21.8 us)
Async XLA Ops:
  0.6 27.6 %collective-permute-start = (bf16[256,2048]{1,0:T(8,128)(2,1)}, bf16[256,2048]{1,0:T(8,128)(2,1)S(1)}, u32[]{:S(2)}, u32[]{:S(2)}) collective-permute-start(bf16[256,2048]{1,0:T(8,128)(2,1)} %bitcast.113), channel_id=1, source_target_pairs={{0,8},{8,16},{16,24},{1,9},{9,17},{17,25},{2,10},{10,18},{18,26},{... | collective-permute-start | bytes 3145736 | tf_op jit(solution)/shard_map/ppermute | solution.py:130
  9.1 19.1 %copy-start = (bf16[1,256,2048]{2,1,0:T(8,128)(2,1)S(1)}, bf16[1,256,2048]{2,1,0:T(8,128)(2,1)}, u32[]{:S(2)}) copy-start(bf16[1,256,2048]{2,1,0:T(8,128)(2,1)} %param.25) | copy-start | bytes 3145732
  9.1 19.1 %copy-start.18 = (bf16[1,256,2048]{2,1,0:T(8,128)(2,1)S(1)}, bf16[1,256,2048]{2,1,0:T(8,128)(2,1)}, u32[]{:S(2)}) copy-start(bf16[1,256,2048]{2,1,0:T(8,128)(2,1)} %param.23) | copy-start | bytes 3145732
  9.1 19.1 %copy-start.19 = (bf16[1,256,2048]{2,1,0:T(8,128)(2,1)S(1)}, bf16[1,256,2048]{2,1,0:T(8,128)(2,1)}, u32[]{:S(2)}) copy-start(bf16[1,256,2048]{2,1,0:T(8,128)(2,1)} %param.22) | copy-start | bytes 3145732
  9.1 19.1 %copy-start.20 = (bf16[1,256,2048]{2,1,0:T(8,128)(2,1)S(1)}, bf16[1,256,2048]{2,1,0:T(8,128)(2,1)}, u32[]{:S(2)}) copy-start(bf16[1,256,2048]{2,1,0:T(8,128)(2,1)} %param.24) | copy-start | bytes 3145732
  28.2 12.2 %copy-start.22 = (bf16[256,2048]{1,0:T(8,128)(2,1)}, bf16[256,2048]{1,0:T(8,128)(2,1)S(1)}, u32[]{:S(2)}) copy-start(bf16[256,2048]{1,0:T(8,128)(2,1)S(1)} %collective-permute-done) | copy-start | bytes 3145732
  40.4 9.5 %copy-start.2 = (pred[256,2048]{1,0:T(8,128)(4,1)}, pred[256,2048]{1,0:T(8,128)(4,1)S(1)}, u32[]{:S(2)}) copy-start(pred[256,2048]{1,0:T(8,128)(4,1)S(1)} %get-tuple-element.11) | copy-start | bytes 1572868
  40.4 9.5 %copy-start.4 = (pred[256,2048]{1,0:T(8,128)(4,1)}, pred[256,2048]{1,0:T(8,128)(4,1)S(1)}, u32[]{:S(2)}) copy-start(pred[256,2048]{1,0:T(8,128)(4,1)S(1)} %get-tuple-element.12) | copy-start | bytes 1572868
  40.4 9.5 %copy-start.6 = (pred[256,2048]{1,0:T(8,128)(4,1)}, pred[256,2048]{1,0:T(8,128)(4,1)S(1)}, u32[]{:S(2)}) copy-start(pred[256,2048]{1,0:T(8,128)(4,1)S(1)} %get-tuple-element.13) | copy-start | bytes 1572868
  40.4 9.5 %copy-start.8 = (pred[256,2048]{1,0:T(8,128)(4,1)}, pred[256,2048]{1,0:T(8,128)(4,1)S(1)}, u32[]{:S(2)}) copy-start(pred[256,2048]{1,0:T(8,128)(4,1)S(1)} %get-tuple-element.14) | copy-start | bytes 1572868
  40.4 9.5 %copy-start.10 = (pred[256,2048]{1,0:T(8,128)(4,1)}, pred[256,2048]{1,0:T(8,128)(4,1)S(1)}, u32[]{:S(2)}) copy-start(pred[256,2048]{1,0:T(8,128)(4,1)S(1)} %get-tuple-element.15) | copy-start | bytes 1572868
  40.5 9.5 %copy-start.12 = (pred[256,2048]{1,0:T(8,128)(4,1)}, pred[256,2048]{1,0:T(8,128)(4,1)S(1)}, u32[]{:S(2)}) copy-start(pred[256,2048]{1,0:T(8,128)(4,1)S(1)} %get-tuple-element.16) | copy-start | bytes 1572868
  40.5 9.5 %copy-start.14 = (pred[256,2048]{1,0:T(8,128)(4,1)}, pred[256,2048]{1,0:T(8,128)(4,1)S(1)}, u32[]{:S(2)}) copy-start(pred[256,2048]{1,0:T(8,128)(4,1)S(1)} %get-tuple-element.17) | copy-start | bytes 1572868
  40.5 9.5 %copy-start.16 = (pred[256,2048]{1,0:T(8,128)(4,1)}, pred[256,2048]{1,0:T(8,128)(4,1)S(1)}, u32[]{:S(2)}) copy-start(pred[256,2048]{1,0:T(8,128)(4,1)S(1)} %get-tuple-element.18) | copy-start | bytes 1572868
  53.6 15.2 %slice-start.2 = ((s8[5505024]{0:T(1024)(128)(4,1)}), s8[4194304]{0:T(1024)(128)(4,1)S(1)}, s32[]{:S(2)}) async-start(s8[5505024]{0:T(1024)(128)(4,1)} %bitcast.123), calls=%async_computation.4 | async-start | bytes 8388608
  54.3 14.5 %slice-start.3 = ((s8[5505024]{0:T(1024)(128)(4,1)}), s8[1310720]{0:T(1024)(128)(4,1)S(1)}, s32[]{:S(2)}) async-start(s8[5505024]{0:T(1024)(128)(4,1)} %bitcast.123), calls=%async_computation.5 | async-start | bytes 2621440
  97.7 60.6 %all-to-all-start = ((bf16[8,168,784]{2,1,0:T(8,128)(2,1)}), bf16[8,168,784]{2,1,0:T(8,128)(2,1)S(1)}, u32[]{:S(2)}, u32[]{:S(2)}) async-start(bf16[8,168,784]{2,1,0:T(8,128)(2,1)} %pad_maximum_fusion.1), calls=%async_computation | async-start | bytes 4816896 | tf_op jit(solution)/shard_map/all_to_all | solution.py:186
  166.7 16.1 %copy-start.34 = (f32[136]{0:T(256)S(1)}, f32[136]{0:T(256)}, u32[]{:S(2)}) copy-start(f32[136]{0:T(256)} %constant.127) | copy-start | bytes 1636
  167.6 15.6 %copy-start.33 = (f32[2,2]{1,0:T(2,128)S(1)}, f32[2,2]{1,0:T(2,128)}, u32[]{:S(2)}) copy-start(f32[2,2]{1,0:T(2,128)} %constant.111.clone) | copy-start | bytes 52
  167.6 16.0 %copy-start.32 = (f32[136]{0:T(256)S(1)}, f32[136]{0:T(256)}, u32[]{:S(2)}) copy-start(f32[136]{0:T(256)} %constant.113.clone) | copy-start | bytes 1636
  167.8 16.0 %copy-start.27 = (bf16[21,8,8,256]{3,2,0,1:T(8,128)(2,1)S(1)}, bf16[21,8,8,256]{3,2,0,1:T(8,128)(2,1)}, u32[]{:S(2)}) copy-start(bf16[21,8,8,256]{3,2,0,1:T(8,128)(2,1)} %copy.37) | copy-start | bytes 2064388
  185.0 42.1 %slice-start.4 = ((s8[5505024]{0:T(1024)(128)(4,1)}), s8[1310720]{0:T(1024)(128)(4,1)S(1)}, s32[]{:S(2)}) async-start(s8[5505024]{0:T(1024)(128)(4,1)} %bitcast.125), calls=%async_computation.6 | async-start | bytes 2621440
  185.0 37.2 %all-to-all-start.1 = ((bf16[8,168,392]{2,1,0:T(8,128)(2,1)}), bf16[8,168,392]{2,1,0:T(8,128)(2,1)S(1)}, u32[]{:S(2)}, u32[]{:S(2)}) async-start(bf16[8,168,392]{2,1,0:T(8,128)(2,1)} %pad_maximum_fusion.2), calls=%async_computation.1 | async-start | bytes 2752512 | tf_op jit(solution)/shard_map/all_to_all | solution.py:248
  189.4 41.0 %collective-permute-start.1 = (bf16[256,2048]{1,0:T(8,128)(2,1)}, bf16[256,2048]{1,0:T(8,128)(2,1)}, u32[]{:S(2)}, u32[]{:S(2)}) collective-permute-start(bf16[256,2048]{1,0:T(8,128)(2,1)} %get-tuple-element.35), channel_id=1, source_target_pairs={{8,0},{16,8},{24,16},{9,1},{17,9},{25,17},{10,2},{18,10},{26,18},{... | collective-permute-start | bytes 3145736 | tf_op jit(solution)/shard_map/ppermute | solution.py:189
  (21 other events, 65.4 us)

commit v2 on v1

--- a/solution.py
+++ b/solution.py
@@ -6,6 +6,8 @@
 import ml_dtypes
 import numpy as np
 from jax import lax
+from jax.experimental import pallas as pl
+from jax.experimental.pallas import tpu as pltpu
 from jax.sharding import PartitionSpec as P
 
 KX = 640
@@ -61,7 +63,13 @@
     wave[-1, 2 * half : 2 * half + 2] = KY
     synth[-1, 2 * half : 2 * half + 2] = 1.0 / count
     wave *= 2.0 * np.pi / (count * GRID_STEP)
-    return half, share, table.reshape(strips * share, count), wave, synth
+    slope = np.zeros((strips, share, count))
+    slope[:, :half] = wave[:, :half, None] * table[:, half : 2 * half]
+    slope[:, half : 2 * half] = -wave[:, half : 2 * half, None] * table[:, :half]
+    slope[:, 2 * half] = wave[:, 2 * half, None] * table[:, 2 * half + 1]
+    slope[:, 2 * half + 1] = -wave[:, 2 * half + 1, None] * table[:, 2 * half]
+    flat = (strips * share, count)
+    return half, share, table.reshape(flat), slope.reshape(flat), wave, synth
 
 
 def x_band(count):
@@ -101,18 +109,54 @@
     return slope[shift], keep[shift], np.cos(ends), np.sin(ends), KX * unit
 
 
-def swap_scaled(array, half, wave):
-    cos_part = array[..., :half, :]
-    sin_part = array[..., half : 2 * half, :]
-    cos_end = array[..., 2 * half : 2 * half + 1, :]
-    sin_end = array[..., 2 * half + 1 : 2 * half + 2, :]
-    rest = array[..., 2 * half + 2 :, :]
-    swapped = jnp.concatenate([sin_part, -cos_part, sin_end, -cos_end, rest], axis=-2)
-    return swapped * wave
-
-
 def dot(a, b, dims):
     return lax.dot_general(a, b, (dims, ((), ())), preferred_element_type=F32)
+
+
+def drag_kernel(level, area, wall_heat, u, v, c, heights, classes, fu, fv, us, vs, heating):
+    rows, columns = u.shape
+    lanes = min(512, columns)
+    for r in range(0, rows, 16):
+        for q in range(0, columns, lanes):
+            at = (slice(r, r + 16), slice(q, q + lanes))
+            kind = classes[at]
+            density = jnp.full(kind.shape, area[0], F32)
+            heat = jnp.full(kind.shape, wall_heat[0], F32)
+            for k in range(1, area.shape[0]):
+                match = kind == k
+                density = jnp.where(match, area[k], density)
+                heat = jnp.where(match, wall_heat[k], heat)
+            inside = level[0] < heights[at]
+            east, north = u[at].astype(F32), v[at].astype(F32)
+            tracer = c[at].astype(F32)
+            speed = jnp.sqrt(east * east + north * north + GUST_FLOOR)
+            drag = 1.0 + jnp.where(inside, DRAG_STEP * density * speed, 0.0)
+            inverse = 1.0 / drag
+            east, north = east * inverse, north * inverse
+            fu[at] = (east * tracer).astype(BF)
+            fv[at] = (north * tracer).astype(BF)
+            us[at] = east.astype(BF)
+            vs[at] = north.astype(BF)
+            heating[at] = jnp.where(inside, heat, 0.0)
+
+
+def drag_fields(level, area, wall_heat, u, v, c, heights, classes):
+    rows, columns = u.shape
+    block = min(64, rows)
+    small = pl.BlockSpec(memory_space=pltpu.SMEM)
+    strip = pl.BlockSpec((block, columns), lambda i: (i, 0))
+    shape = lambda dtype: jax.ShapeDtypeStruct((rows, columns), dtype)
+    return pl.pallas_call(
+        drag_kernel,
+        grid=(rows // block,),
+        in_specs=[small] * 3 + [strip] * 5,
+        out_specs=[strip] * 5,
+        out_shape=[shape(BF)] * 4 + [shape(F32)],
+        compiler_params=pltpu.CompilerParams(vmem_limit_bytes=40 * 2**20),
+        cost_estimate=pl.CostEstimate(
+            flops=60 * rows * columns, bytes_accessed=26 * rows * columns, transcendentals=0
+        ),
+    )(level, area, wall_heat, u, v, c, heights, classes)
 
 
 def per_device(tables, u_wind, v_wind, w_wind, scalar, heights, wall_class, wall_area, wall_heat):
@@ -128,67 +172,40 @@
     up = [(i, i + 1) for i in range(groups - 1)]
     down = [(i + 1, i) for i in range(groups - 1)]
     c_below = lax.ppermute(c_flat, "gz", up)
-
-    inside = level < heights
-    density = jnp.zeros(heights.shape, F32)
-    heat = jnp.zeros(heights.shape, F32)
-    for k in range(wall_area.shape[0]):
-        match = wall_class == k
-        density = jnp.where(match, wall_area[k], density)
-        heat = jnp.where(match, wall_heat[k], heat)
-    east, north = u_wind[0].astype(F32), v_wind[0].astype(F32)
-    tracer = c_flat.astype(F32)
-    speed = jnp.sqrt(east * east + north * north + GUST_FLOOR)
-    drag = 1.0 + jnp.where(inside, DRAG_STEP * density * speed, 0.0)
-    east_star = east / drag
-    north_star = north / drag
-    heating = jnp.where(inside, heat, 0.0)
+    flux_u, flux_v, u_bf, v_bf, heating = drag_fields(
+        level.reshape(1), wall_area, wall_heat, u_wind[0], v_wind[0], c_flat, heights, wall_class
+    )
+
+    mn, nt, tn = ((1,), (0,)), ((1,), (1,)), ((0,), (0,))
+    y_high, y_low = tables["y"]
+    s_high, s_low = tables["y_slope"]
+    exchange = partial(lax.all_to_all, axis_name="xy", split_axis=0, concat_axis=0, tiled=True)
+    blocks = lambda t: t.reshape(strips, share, -1).astype(BF)
+    z_east = exchange(blocks(dot(y_high, flux_u, nt)))
 
     first_row = strip * row_count
     rows = lambda t: lax.dynamic_slice_in_dim(t, first_row, row_count, 1)
     basis = jnp.concatenate([rows(tables["basis"][0]), rows(tables["basis"][1])], axis=1)
     slope = jnp.concatenate([rows(tables["slope"][0]), rows(tables["slope"][1])], axis=1)
-    mn = ((1,), (0,))
-
-    def low_modes(table, field):
-        high, low = split(field)
-        return dot(table, jnp.concatenate([high, high], axis=0), mn) + dot(
-            table[:, :row_count], low, mn
-        )
-
-    w_modes = dot(basis, jnp.concatenate([w_flat, w_flat], axis=0), mn) * (1.0 / LEVEL_STEP)
-    a_modes = low_modes(slope, east_star) - w_modes
-    b_modes = low_modes(basis, north_star)
-    modes_high, modes_low = split(jnp.concatenate([a_modes, w_modes, b_modes], axis=0))
-    fields = jnp.concatenate(
-        [
-            (east_star * tracer).astype(BF),
-            (north_star * tracer).astype(BF),
-            modes_high,
-            modes_low,
-        ],
-        axis=0,
-    )
-    y_high, y_low = tables["y"]
-    nt = ((1,), (1,))
-    spectra = dot(y_high, fields, nt)
-    low = dot(y_low, modes_high, nt)
-    spectra = spectra.reshape(strips, share, -1)
-    low = low.reshape(strips, share, -1)
-    first = 2 * row_count
-    press = spectra[..., first : first + 3 * width] + spectra[..., first + 3 * width :] + low
-    wave_y = jnp.asarray(tables["wave_y"], F32)[..., None]
-    flux_v = swap_scaled(spectra[..., row_count : 2 * row_count], half, wave_y)
-    rhs_part = press[..., :width] + swap_scaled(press[..., 2 * width :], half, wave_y)
-    sent = jnp.concatenate(
-        [spectra[..., :row_count], flux_v, rhs_part, press[..., width : 2 * width]], axis=-1
-    ).astype(BF)
-    got = lax.all_to_all(sent, "xy", split_axis=0, concat_axis=0, tiled=True)
-
+    low_modes = lambda table, field: dot(table, jnp.concatenate([field, field], axis=0), mn)
+    w_modes = low_modes(basis, w_flat) * (1.0 / LEVEL_STEP)
+    a_modes = low_modes(slope, u_bf) - w_modes
+    b_modes = low_modes(basis, v_bf)
+
+    def three(high, low, modes):
+        m_high, m_low = split(modes)
+        return dot(high, m_high, nt) + dot(high, m_low, nt) + dot(low, m_high, nt)
+
+    rhs_part = three(y_high, y_low, a_modes) + three(s_high, s_low, b_modes)
+    low_part = three(y_high, y_low, w_modes)
+    got = exchange(blocks(jnp.concatenate([rhs_part, low_part], axis=1)))
+    z_north = exchange(blocks(dot(s_high, flux_v, nt)))
+
+    tracer = c_flat.astype(F32)
     flux = w_flat.astype(F32) * (tracer + c_below.astype(F32)) * (0.5 / LEVEL_STEP)
     flux_above = lax.ppermute(flux.astype(BF), "gz", down)
 
-    sums = jnp.sum(got[..., 2 * row_count :].astype(F32), axis=0)
+    sums = jnp.sum(got.astype(F32), axis=0)
     all_sums = lax.all_gather(sums, "gz", axis=0, tiled=False)
     wave_own = lax.dynamic_index_in_dim(
         jnp.asarray(tables["wave_y"], F32), strip, 0, keepdims=False
@@ -223,15 +240,12 @@
     )[:, None]
     own = own * (synth_y * jnp.asarray(tables["synth_x"], F32)[None, :] * tables["gain"])
 
-    z_east = jnp.swapaxes(got[..., :row_count], 0, 1).reshape(share, count_x)
-    z_north = jnp.swapaxes(got[..., row_count : 2 * row_count], 0, 1).reshape(share, count_x)
-    both = jnp.concatenate([z_east, z_north], axis=1)
-    product = dot(both, tables["x_high"], mn)
-    if tables["x_low"] is not None:
-        product = product + dot(both, tables["x_low"], mn)
+    wide = lambda t: jnp.swapaxes(t, 0, 1).reshape(share, count_x)
+    z_east, z_north = wide(z_east), wide(z_north)
+    product = dot(z_east, tables["x_slope"], mn) + dot(z_north, tables["x_keep"], mn)
     ends = jnp.asarray(tables["ends"], F32)
-    pair = both[2 * half : 2 * half + 2].astype(F32)
-    pe, pn = pair[:, :count_x], pair[:, count_x:]
+    pe = z_east[2 * half : 2 * half + 2].astype(F32)
+    pn = z_north[2 * half : 2 * half + 2].astype(F32)
     top = tables["top"]
     ec, es = jnp.sum(pe * ends[0], axis=1), jnp.sum(pe * ends[1], axis=1)
     nc, ns = jnp.sum(pn * ends[0], axis=1), jnp.sum(pn * ends[1], axis=1)
@@ -244,18 +258,10 @@
     )
     product = product * synth_y
     back = jnp.swapaxes(product.reshape(share, strips, row_count), 0, 1).astype(BF)
-    own = jnp.broadcast_to(own.astype(BF)[None], (strips, share, width))
-    returned = lax.all_to_all(
-        jnp.concatenate([back, own], axis=-1), "xy", split_axis=0, concat_axis=0, tiled=True
-    ).reshape(strips * share, row_count + width)
-
-    tn = ((0,), (0,))
-    planes = dot(returned, y_high, tn)
-    if tables["low_back"]:
-        planes = planes + dot(returned, y_low, tn)
-        pressed = planes[row_count:]
-    else:
-        pressed = planes[row_count:] + dot(returned[:, row_count:], y_low, tn)
+    returned = exchange(back).reshape(strips * share, row_count)
+    solved = lax.all_gather(own.astype(BF), "xy", axis=0, tiled=True)
+
+    pressed = dot(solved, y_high, tn) + dot(solved, y_low, tn)
     p_high, p_low = split(pressed)
     b_high, b_low = rows(tables["basis"][0]), rows(tables["basis"][1])
     pressure = dot(
@@ -264,11 +270,8 @@
         tn,
     ) * (1.0 / tables["gain"])
     vertical = flux_above.astype(F32) - flux
-    tendency = (heating - planes[:row_count] - vertical).astype(BF)
+    tendency = (heating - dot(returned, y_high, tn) - vertical).astype(BF)
     return (tendency[None], pressure[None])
-
-
-OPTIONS = {"low_back": False, "x_low": False}
 
 
 def solution(mesh):
@@ -276,15 +279,15 @@
     def whole(u_wind, *others):
         _, count_x, count_y = u_wind.shape
         strips = mesh.shape["xy"]
-        half, share, y_table, wave_y, synth_y = y_layout(strips, count_y)
+        half, share, y_table, y_slope, wave_y, synth_y = y_layout(strips, count_y)
         width, basis, slope, wave_x, synth_x = x_band(count_x)
         x_slope, x_keep, end_cos, end_sin, top = x_operators(count_x)
-        x_high, x_low = split_np(np.concatenate([x_slope, x_keep], axis=0))
         tables = {
             "half": half,
             "share": share,
             "width": width,
             "y": split_np(y_table),
+            "y_slope": split_np(y_slope),
             "wave_y": wave_y,
             "synth_y": synth_y,
             "basis": split_np(basis),
@@ -292,11 +295,10 @@
             "wave_x": wave_x,
             "synth_x": synth_x,
             "gain": float(count_x),
-            "x_high": x_high,
-            "x_low": x_low if OPTIONS["x_low"] else None,
+            "x_slope": x_slope.astype(ml_dtypes.bfloat16),
+            "x_keep": x_keep.astype(ml_dtypes.bfloat16),
             "ends": np.stack([end_cos, end_sin]),
             "top": top,
-            "low_back": OPTIONS["low_back"],
         }
         return jax.shard_map(
             partial(per_device, tables),

time: 243 us -> 167 us (0.69)
  waiting for transfers between devices: 103 us -> 13.8 us
  other arithmetic: 46.2 us -> 12.3 us
  matrix products: 36.3 us -> 55.8 us
  blocking collectives: 15 us -> 30.5 us
  starting transfers between devices: 14.8 us -> 25.7 us
  Pallas kernels: 0 us -> 4.48 us
  local copies, waits for them, and re-layouts: 24.6 us -> 21.5 us
    all_to_all x2 -> x4, waiting for transfers between devices: 86.6 us -> 13.8 us  [the longest x1 12.6 us: per_device(): got = exchange(blocks(jnp.concatenate([rhs_part, low_part], axis=1)))]
    convert_element_type x7 -> x1, other arithmetic: 22.5 us -> 3.05 us  [per_device(): flux_above = lax.ppermute(flux.astype(BF), 'gz', down)]
    dot_general x12 -> x20, matrix products: 36.3 us -> 55.8 us  [dot(): return lax.dot_general(a, b, (dims, ((), ())), preferred_element_type=F32)]
    ppermute x1, waiting for transfers between devices: 16.9 us -> 0.01 us  [per_device(): c_below = lax.ppermute(c_flat, 'gz', up)]
    all_gather x0 -> x1, blocking collectives: none -> 15 us  [per_device(): solved = lax.all_gather(own.astype(BF), 'xy', axis=0, tiled=True)]
    concatenate x2 -> x0, local copies, waits for them, and re-layouts: 13.8 us -> none  [swap_scaled(): jnp.concatenate([sin_part, -cos_part, sin_end, -cos_end, rest], axis=-2)]
    all_to_all x2 -> x4, starting transfers between devices: 8.59 us -> 18.6 us  [the longest x1 5.23 us: per_device(): z_north = exchange(blocks(dot(s_high, flux_v, nt)))]
    unnamed x83 -> x70, local copies, waits for them, and re-layouts: 2.28 us -> 11.2 us
  transfers between devices with their start and end apart: 4 -> 6, of which waited for: 3 -> 2; matrix products, arithmetic and copies ran while one was open for 6% -> 46% of each run, Pallas kernels for 0% -> 3%
where the time goes in v2:
time: 167 us; the launch traced here: 165 us
  matrix products  55.8 us (33%)
  blocking collectives  30.5 us (18%)
  starting transfers between devices  25.7 us (15%)
  local copies, waits for them, and re-layouts  21.5 us (13%)
  waiting for transfers between devices  13.8 us (8%)
  other arithmetic  12.3 us (7%)
  Pallas kernels  4.48 us (3%)
    dot_general x20, matrix products, dot(): return lax.dot_general(a, b, (dims, ((), ())), preferred_element_type=F32)  55.8 us
    all_gather x1, blocking collectives, per_device(): all_sums = lax.all_gather(sums, 'gz', axis=0, tiled=False)  15.5 us
    all_gather x1, blocking collectives, per_device(): solved = lax.all_gather(own.astype(BF), 'xy', axis=0, tiled=True)  15 us
    all_to_all x1, waiting for transfers between devices, per_device(): got = exchange(blocks(jnp.concatenate([rhs_part, low_part], axis=1)))  12.6 us
    unnamed x70, local copies, waits for them, and re-layouts  11.2 us
    ppermute x1, starting transfers between devices, per_device(): c_below = lax.ppermute(c_flat, 'gz', up)  5.85 us
    all_to_all x1, starting transfers between devices, per_device(): z_north = exchange(blocks(dot(s_high, flux_v, nt)))  5.23 us
    all_to_all x1, starting transfers between devices, per_device(): z_east = exchange(blocks(dot(y_high, flux_u, nt)))  4.88 us
  transfers between devices with their start and end apart: 6, of which 2 were waited for; matrix products, arithmetic and copies ran while one was open for 46% of the time, Pallas kernels for 3%

profile of v2, /device:TPU:0, one launch (start us, length us, event | category | flops | bytes accessed | tf_op | source)
XLA Modules:
  0.0 165.4 jit_solution(1885683354531006859)
XLA Ops:
  0.6 5.8 %collective-permute-start = (bf16[256,2048]{1,0:T(8,128)(2,1)}, bf16[256,2048]{1,0:T(8,128)(2,1)}, u32[]{:S(2)}, u32[]{:S(2)}) collective-permute-start(bf16[256,2048]{1,0:T(8,128)(2,1)} %bitcast.100), channel_id=1, source_target_pairs={{0,8},{8,16},{16,24},{1,9},{9,17},{17,25},{2,10},{10,18},{18,26},{... | collective-permute-start | bytes 3145736 | tf_op jit(solution)/shard_map/ppermute | solution.py:174
  14.7 4.5 %shard_map.239 = (bf16[256,2048]{1,0:T(8,128)(2,1)S(1)}, bf16[256,2048]{1,0:T(8,128)(2,1)S(1)}, bf16[256,2048]{1,0:T(8,128)(2,1)S(1)}, bf16[256,2048]{1,0:T(8,128)(2,1)S(1)}, f32[256,2048]{1,0:T(8,128)S(1)}) custom-call(s32[1]{0:T(128)} %bitcast.level, f32[8]{0:T(128)S(1)} %copy-done.6, f32[8]{0:T(128)S(1)} %copy-done.7, bf16[256,2048]{1,0:T(8,128)(2,1)S(1)} %bitcast.102, ...), custom_call_target="tpu_custom_call" | custom-call | flops 31457280 | bytes 13631488 | tf_op jit(solution)/shard_map/pallas_call | solution.py:149
  19.2 2.5 %convolution_convert_fusion.1 = bf16[256,1344]{0,1:T(8,128)(2,1)} fusion(bf16[256,2048]{1,0:T(8,128)(2,1)S(1)} %get-tuple-element.8, bf16[1344,2048]{1,0:T(8,128)(2,1)S(1)} %copy-done.12), kind=kOutput, calls=%fused_computation.4 | convolution fusion | flops 1409630208 | bytes 7241728 | tf_op jit(solution)/shard_map/dot_general | solution.py:113
  21.7 4.9 %all-to-all-start = ((bf16[8,168,256]{2,1,0:T(8,128)(2,1)}), bf16[8,168,256]{2,1,0:T(8,128)(2,1)}, u32[]{:S(2)}, u32[]{:S(2)}) async-start(bf16[8,168,256]{2,1,0:T(8,128)(2,1)} %bitcast.117), calls=%async_computation | async-start | bytes 1376256 | tf_op jit(solution)/shard_map/all_to_all | solution.py:184
  28.5 2.2 %convolution_multiply_fusion.1 = f32[136,2048]{1,0:T(8,128)S(1)} fusion(bf16[256,2048]{1,0:T(8,128)(2,1)} %bitcast.113, bf16[136,256]{1,0:T(8,128)(2,1)S(1)} %get-tuple-element.26, bf16[136,256]{1,0:T(8,128)(2,1)S(1)} %get-tuple-element.27), kind=kOutput, calls=%fused_computation.5 | convolution fusion | flops 289964032 | bytes 2301952 | tf_op jit(solution)/shard_map/dot_general | solution.py:113
  43.0 2.8 %fusion.5 = bf16[1344,136]{0,1:T(8,128)(2,1)} fusion(f32[136,1344]{1,0:T(8,128)S(1)} %convolution_add_fusion.4, f32[136,1344]{1,0:T(8,128)S(1)} %convolution_add_fusion.3, bf16[1344,2048]{1,0:T(8,128)(2,1)S(1)} %bitcast.109, f32[136,2048]{1,0:T(8,128)S(1)} %fusion.12), kind=kOutput, calls=%fused_computation.19 | convolution fusion | flops 749788672 | bytes 8446976 | tf_op jit(solution)/shard_map/dot_general | solution.py:113
  47.8 2.8 %convolution_convert_fusion = bf16[256,1344]{0,1:T(8,128)(2,1)} fusion(bf16[256,2048]{1,0:T(8,128)(2,1)S(1)} %get-tuple-element.9, bf16[1344,2048]{1,0:T(8,128)(2,1)S(1)} %bitcast.107), kind=kOutput, calls=%fused_computation.3 | convolution fusion | flops 1409630208 | bytes 7241728 | tf_op jit(solution)/shard_map/dot_general | solution.py:113
  50.6 2.9 %convolution_add_fusion.1 = f32[136,1344]{1,0:T(8,128)} fusion(f32[136,1344]{1,0:T(8,128)S(1)} %fusion.32, bf16[1344,2048]{1,0:T(8,128)(2,1)S(1)} %copy-done.13, f32[136,2048]{1,0:T(8,128)S(1)} %convolution_multiply_fusion.1), kind=kOutput, calls=%fused_computation.8 | convolution fusion | flops 749701632 | bytes 8081408 | tf_op jit(solution)/shard_map/dot_general | solution.py:113
  53.4 5.2 %all-to-all-start.1 = ((bf16[8,168,256]{2,1,0:T(8,128)(2,1)}), bf16[8,168,256]{2,1,0:T(8,128)(2,1)}, u32[]{:S(2)}, u32[]{:S(2)}) async-start(bf16[8,168,256]{2,1,0:T(8,128)(2,1)} %bitcast.118), calls=%async_computation.1 | async-start | bytes 1376256 | tf_op jit(solution)/shard_map/all_to_all | solution.py:202
  58.7 5.5 %fusion.4 = bf16[1344,136]{0,1:T(8,128)(2,1)} fusion(f32[136,1344]{1,0:T(8,128)} %convolution_add_fusion.1, bf16[1344,2048]{1,0:T(8,128)(2,1)} %constant.97.clone, f32[136,2048]{1,0:T(8,128)S(1)} %copy-done.15), kind=kOutput, calls=%fused_computation.18 | convolution fusion | flops 749605888 | bytes 7715840 | tf_op jit(solution)/shard_map/dot_general | solution.py:113
  64.2 2.1 %pad_maximum_fusion = bf16[1344,272]{0,1:T(8,128)(2,1)} fusion(bf16[1344,136]{0,1:T(8,128)(2,1)} %fusion.4, bf16[1344,136]{0,1:T(8,128)(2,1)} %fusion.5), kind=kLoop, calls=%fused_computation.53 | loop fusion | flops 1462272 | bytes 1462272 | tf_op jit(solution)/shard_map/concatenate | solution.py:201
  66.3 2.3 %copy.57 = bf16[1344,272]{1,0:T(8,128)(2,1)} copy(bf16[1344,272]{0,1:T(8,128)(2,1)} %pad_maximum_fusion) | data formatting | bytes 1462272 | tf_op jit(solution)/shard_map/convert_element_type | solution.py:183
  70.0 3.1 %fusion.21 = bf16[256,2048]{1,0:T(8,128)(2,1)} fusion(bf16[256,2048]{1,0:T(8,128)(2,1)} %collective-permute-done, bf16[1,256,2048]{2,1,0:T(8,128)(2,1)} %param.26, bf16[1,256,2048]{2,1,0:T(8,128)(2,1)S(1)} %copy-done.1), kind=kLoop, calls=%fused_computation.47 | loop fusion | flops 3670016 | bytes 4194304 | tf_op jit(solution)/shard_map/convert_element_type | solution.py:206
  77.6 4.2 %all-to-all-start.3 = ((bf16[8,168,272]{2,1,0:T(8,128)(2,1)}), bf16[8,168,272]{2,1,0:T(8,128)(2,1)}, u32[]{:S(2)}, u32[]{:S(2)}) async-start(bf16[8,168,272]{2,1,0:T(8,128)(2,1)} %bitcast.114), calls=%async_computation.3 | async-start | bytes 2064384 | tf_op jit(solution)/shard_map/all_to_all | solution.py:201
  83.1 5.2 %fusion.66 = f32[168,2048]{1,0:T(8,128)S(1)} fusion(bf16[168,2048]{1,0:T(8,128)(2,1)} %bitcast.111, bf16[2048,2048]{1,0:T(8,128)(2,1)} %constant.105.clone), kind=kOutput, calls=%fused_computation.119 | convolution fusion | flops 1409286144 | bytes 10452992 | tf_op jit(solution)/shard_map/dot_general | solution.py:113
  88.3 5.1 %convolution_add_fusion.6 = f32[168,2048]{1,0:T(8,128)S(1)} fusion(f32[168,2048]{1,0:T(8,128)S(1)} %fusion.66, bf16[168,2048]{1,0:T(8,128)(2,1)S(1)} %bitcast.112, bf16[2048,2048]{1,0:T(8,128)(2,1)} %constant.106.clone), kind=kOutput, calls=%fused_computation.14 | convolution fusion | flops 1409630208 | bytes 11829248 | tf_op jit(solution)/shard_map/dot_general | solution.py:113
  95.6 12.6 %all-to-all-done.3 = bf16[8,168,272]{2,1,0:T(8,128)(2,1)} async-done(((bf16[8,168,272]{2,1,0:T(8,128)(2,1)}), bf16[8,168,272]{2,1,0:T(8,128)(2,1)}, u32[]{:S(2)}, u32[]{:S(2)}) %all-to-all-start.3) | async-done | bytes 731168 | tf_op jit(solution)/shard_map/all_to_all | solution.py:201
  108.1 4.2 %all-to-all-start.2 = ((bf16[8,168,256]{2,1,0:T(8,128)(2,1)}), bf16[8,168,256]{2,1,0:T(8,128)(2,1)}, u32[]{:S(2)}, u32[]{:S(2)}) async-start(bf16[8,168,256]{2,1,0:T(8,128)(2,1)} %bitcast.116), calls=%async_computation.2 | async-start | bytes 1376256 | tf_op jit(solution)/shard_map/all_to_all | solution.py:261
  113.8 15.5 %all-gather = f32[672,272]{1,0:T(8,128)S(1)} all-gather(f32[168,272]{1,0:T(8,128)S(1)} %convert_reduce_fusion), channel_id=2, replica_groups=mesh['gz'=4,'xy'=8] {'gz'}, dimensions={0}, use_global_device_ids=true | all-gather | bytes 913920 | tf_op jit(solution)/shard_map/all_gather | solution.py:209
  130.3 15.0 %all-gather.1 = bf16[8,168,136]{1,2,0:T(8,128)(2,1)S(1)} all-gather(bf16[1,168,136]{1,2,0:T(8,128)(2,1)S(1)} %copy.55), channel_id=1, replica_groups=mesh['gz'=4,'xy'=8] {'xy'}, dimensions={0}, use_global_device_ids=true | all-gather | bytes 411264 | tf_op jit(solution)/shard_map/all_gather | solution.py:262
  147.8 3.6 %fusion.67 = f32[136,2048]{1,0:T(8,128)S(1)} fusion(bf16[1344,136]{0,1:T(8,128)(2,1)S(1)} %reshape.80, bf16[1344,2048]{1,0:T(8,128)(2,1)} %constant.92.clone), kind=kOutput, calls=%fused_computation.120 | convolution fusion | flops 748683264 | bytes 6984704 | tf_op jit(solution)/shard_map/dot_general | solution.py:113
  151.5 3.7 %reduce-precision_convert_fusion = (bf16[136,2048]{1,0:T(8,128)(2,1)S(1)}, bf16[136,2048]{1,0:T(8,128)(2,1)S(1)}) fusion(f32[136,2048]{1,0:T(8,128)S(1)} %fusion.67, bf16[1344,136]{0,1:T(8,128)(2,1)S(1)} %reshape.80, bf16[1344,2048]{1,0:T(8,128)(2,1)} %constant.97.clone), kind=kOutput, calls=%fused_computation.39 | convolution fusion | flops 750075904 | bytes 8098816 | tf_op jit(solution)/shard_map/dot_general | solution.py:113
  157.3 4.7 %convolution_subtract_fusion = f32[256,2048]{1,0:T(8,128)S(1)} fusion(f32[256,2048]{1,0:T(8,128)S(1)} %get-tuple-element.7, bf16[1344,256]{1,0:T(8,128)(2,1)} %bitcast.12, bf16[1344,2048]{1,0:T(8,128)(2,1)} %constant.92.clone), kind=kOutput, calls=%fused_computation.2 | convolution fusion | flops 1409810432 | bytes 10387456 | tf_op jit(solution)/shard_map/dot_general | solution.py:113
  162.0 3.4 %fusion.26 = bf16[1,256,2048]{2,1,0:T(8,128)(2,1)} fusion(f32[256,2048]{1,0:T(8,128)S(1)} %convolution_subtract_fusion, bf16[256,2048]{1,0:T(8,128)(2,1)} %collective-permute-done, bf16[256,2048]{1,0:T(8,128)(2,1)} %collective-permute-done.1, bf16[1,256,2048]{2,1,0:T(8,128)(2,1)S(1)} %copy-done.16, bf16[1,256,2048]{2,1,0:T(8,128)(2,1)S(1)} %copy-done.1), kind=kLoop, calls=%fused_computation.52 | loop fusion | flops 5242880 | bytes 7340032 | tf_op jit(solution)/shard_map/broadcast_in_dim | solution.py:274
  (109 shorter events, 40.6 us)
Async XLA Ops:
  0.6 69.3 %collective-permute-start = (bf16[256,2048]{1,0:T(8,128)(2,1)}, bf16[256,2048]{1,0:T(8,128)(2,1)}, u32[]{:S(2)}, u32[]{:S(2)}) collective-permute-start(bf16[256,2048]{1,0:T(8,128)(2,1)} %bitcast.100), channel_id=1, source_target_pairs={{0,8},{8,16},{16,24},{1,9},{9,17},{17,25},{2,10},{10,18},{18,26},{... | collective-permute-start | bytes 3145736 | tf_op jit(solution)/shard_map/ppermute | solution.py:174
  14.7 4.5 %copy-start.12 = (bf16[1344,2048]{1,0:T(8,128)(2,1)S(1)}, bf16[1344,2048]{1,0:T(8,128)(2,1)}, u32[]{:S(2)}) copy-start(bf16[1344,2048]{1,0:T(8,128)(2,1)} %constant.92.clone) | copy-start | bytes 16515076
  21.7 31.8 %all-to-all-start = ((bf16[8,168,256]{2,1,0:T(8,128)(2,1)}), bf16[8,168,256]{2,1,0:T(8,128)(2,1)}, u32[]{:S(2)}, u32[]{:S(2)}) async-start(bf16[8,168,256]{2,1,0:T(8,128)(2,1)} %bitcast.117), calls=%async_computation | async-start | bytes 1376256 | tf_op jit(solution)/shard_map/all_to_all | solution.py:184
  27.5 8.9 %copy-start.17 = (bf16[136,256]{1,0:T(8,128)(2,1)}, bf16[136,256]{1,0:T(8,128)(2,1)S(1)}, u32[]{:S(2)}) copy-start(bf16[136,256]{1,0:T(8,128)(2,1)S(1)} %get-tuple-element.26) | copy-start | bytes 208900
  27.5 8.9 %copy-start.19 = (bf16[136,256]{1,0:T(8,128)(2,1)}, bf16[136,256]{1,0:T(8,128)(2,1)S(1)}, u32[]{:S(2)}) copy-start(bf16[136,256]{1,0:T(8,128)(2,1)S(1)} %get-tuple-element.27) | copy-start | bytes 208900
  28.5 3.9 %copy-start.13 = (bf16[1344,2048]{1,0:T(8,128)(2,1)S(1)}, bf16[1344,2048]{1,0:T(8,128)(2,1)}, u32[]{:S(2)}) copy-start(bf16[1344,2048]{1,0:T(8,128)(2,1)} %constant.92.clone) | copy-start | bytes 16515076
  30.7 19.9 %copy-start.14 = (f32[136,2048]{1,0:T(8,128)}, f32[136,2048]{1,0:T(8,128)S(1)}, u32[]{:S(2)}) copy-start(f32[136,2048]{1,0:T(8,128)S(1)} %convolution_multiply_fusion.1) | copy-start | bytes 3342340
  32.4 4.5 %slice-start.2 = ((s8[5505024]{0:T(1024)(128)(4,1)}), s8[4194304]{0:T(1024)(128)(4,1)S(1)}, s32[]{:S(2)}) async-start(s8[5505024]{0:T(1024)(128)(4,1)} %bitcast.106), calls=%async_computation.6 | async-start | bytes 8388608
  37.0 4.0 %slice-start = ((s8[5505024]{0:T(1024)(128)(4,1)}), s8[4194304]{0:T(1024)(128)(4,1)S(1)}, s32[]{:S(2)}) async-start(s8[5505024]{0:T(1024)(128)(4,1)} %bitcast.104), calls=%async_computation.4 | async-start | bytes 8388608
  39.0 4.0 %slice-start.4 = ((s8[5505024]{0:T(1024)(128)(4,1)}), s8[4194304]{0:T(1024)(128)(4,1)S(1)}, s32[]{:S(2)}) async-start(s8[5505024]{0:T(1024)(128)(4,1)} %bitcast.108), calls=%async_computation.8 | async-start | bytes 8388608
  53.4 5.2 %copy-start.15 = (f32[136,2048]{1,0:T(8,128)S(1)}, f32[136,2048]{1,0:T(8,128)}, u32[]{:S(2)}) copy-start(f32[136,2048]{1,0:T(8,128)} %copy-done.14) | copy-start | bytes 3342340
  53.4 24.2 %all-to-all-start.1 = ((bf16[8,168,256]{2,1,0:T(8,128)(2,1)}), bf16[8,168,256]{2,1,0:T(8,128)(2,1)}, u32[]{:S(2)}, u32[]{:S(2)}) async-start(bf16[8,168,256]{2,1,0:T(8,128)(2,1)} %bitcast.118), calls=%async_computation.1 | async-start | bytes 1376256 | tf_op jit(solution)/shard_map/all_to_all | solution.py:202
  64.2 5.8 %copy-start.1 = (bf16[1,256,2048]{2,1,0:T(8,128)(2,1)S(1)}, bf16[1,256,2048]{2,1,0:T(8,128)(2,1)}, u32[]{:S(2)}) copy-start(bf16[1,256,2048]{2,1,0:T(8,128)(2,1)} %param.27) | copy-start | bytes 3145732
  73.0 89.0 %collective-permute-start.1 = (bf16[256,2048]{1,0:T(8,128)(2,1)}, bf16[256,2048]{1,0:T(8,128)(2,1)}, u32[]{:S(2)}, u32[]{:S(2)}) collective-permute-start(bf16[256,2048]{1,0:T(8,128)(2,1)} %fusion.21), channel_id=1, source_target_pairs={{8,0},{16,8},{24,16},{9,1},{17,9},{25,17},{10,2},{18,10},{26,18},{... | collective-permute-start | bytes 3145736 | tf_op jit(solution)/shard_map/ppermute | solution.py:206
  77.6 30.5 %all-to-all-start.3 = ((bf16[8,168,272]{2,1,0:T(8,128)(2,1)}), bf16[8,168,272]{2,1,0:T(8,128)(2,1)}, u32[]{:S(2)}, u32[]{:S(2)}) async-start(bf16[8,168,272]{2,1,0:T(8,128)(2,1)} %bitcast.114), calls=%async_computation.3 | async-start | bytes 2064384 | tf_op jit(solution)/shard_map/all_to_all | solution.py:201
  88.3 5.1 %copy-start.21 = (f32[8,256]{1,0:T(8,128)S(1)}, f32[8,256]{1,0:T(8,128)}, u32[]{:S(2)}) copy-start(f32[8,256]{1,0:T(8,128)} %constant.113) | copy-start | bytes 24580
  88.3 5.1 %copy-start.22 = (f32[8,256]{1,0:T(8,128)S(1)}, f32[8,256]{1,0:T(8,128)}, u32[]{:S(2)}) copy-start(f32[8,256]{1,0:T(8,128)} %constant.115) | copy-start | bytes 24580
  88.3 6.1 %copy-start.23 = (f32[2048]{0:T(1024)S(1)}, f32[2048]{0:T(1024)}, u32[]{:S(2)}) copy-start(f32[2048]{0:T(1024)} %constant.116) | copy-start | bytes 24580
  88.3 6.1 %copy-start.24 = (f32[2048]{0:T(1024)S(1)}, f32[2048]{0:T(1024)}, u32[]{:S(2)}) copy-start(f32[2048]{0:T(1024)} %constant.117) | copy-start | bytes 24580
  95.6 33.7 %copy-start.27 = (f32[136]{0:T(256)S(1)}, f32[136]{0:T(256)}, u32[]{:S(2)}) copy-start(f32[136]{0:T(256)} %constant.119) | copy-start | bytes 1636
  108.1 49.2 %all-to-all-start.2 = ((bf16[8,168,256]{2,1,0:T(8,128)(2,1)}), bf16[8,168,256]{2,1,0:T(8,128)(2,1)}, u32[]{:S(2)}, u32[]{:S(2)}) async-start(bf16[8,168,256]{2,1,0:T(8,128)(2,1)} %bitcast.116), calls=%async_computation.2 | async-start | bytes 1376256 | tf_op jit(solution)/shard_map/all_to_all | solution.py:261
  112.3 17.4 %copy-start.26 = (f32[2,2]{1,0:T(2,128)S(1)}, f32[2,2]{1,0:T(2,128)}, u32[]{:S(2)}) copy-start(f32[2,2]{1,0:T(2,128)} %constant.102.clone) | copy-start | bytes 52
  112.4 17.8 %copy-start.25 = (f32[136]{0:T(256)S(1)}, f32[136]{0:T(256)}, u32[]{:S(2)}) copy-start(f32[136]{0:T(256)} %constant.104.clone) | copy-start | bytes 1636
  157.3 4.7 %copy-start.16 = (bf16[1,256,2048]{2,1,0:T(8,128)(2,1)S(1)}, bf16[1,256,2048]{2,1,0:T(8,128)(2,1)}, u32[]{:S(2)}) copy-start(bf16[1,256,2048]{2,1,0:T(8,128)(2,1)} %param.26) | copy-start | bytes 3145732
  (16 other events, 31.6 us)

commit v3 on v2

--- a/solution.py
+++ b/solution.py
@@ -152,7 +152,7 @@
         in_specs=[small] * 3 + [strip] * 5,
         out_specs=[strip] * 5,
         out_shape=[shape(BF)] * 4 + [shape(F32)],
-        compiler_params=pltpu.CompilerParams(vmem_limit_bytes=40 * 2**20),
+        compiler_params=pltpu.CompilerParams(vmem_limit_bytes=60 * 2**20),
         cost_estimate=pl.CostEstimate(
             flops=60 * rows * columns, bytes_accessed=26 * rows * columns, transcendentals=0
         ),
@@ -171,7 +171,6 @@
     w_flat, c_flat = w_wind[0], scalar[0]
     up = [(i, i + 1) for i in range(groups - 1)]
     down = [(i + 1, i) for i in range(groups - 1)]
-    c_below = lax.ppermute(c_flat, "gz", up)
     flux_u, flux_v, u_bf, v_bf, heating = drag_fields(
         level.reshape(1), wall_area, wall_heat, u_wind[0], v_wind[0], c_flat, heights, wall_class
     )
@@ -181,7 +180,15 @@
     s_high, s_low = tables["y_slope"]
     exchange = partial(lax.all_to_all, axis_name="xy", split_axis=0, concat_axis=0, tiled=True)
     blocks = lambda t: t.reshape(strips, share, -1).astype(BF)
-    z_east = exchange(blocks(dot(y_high, flux_u, nt)))
+    east_spectra = blocks(dot(y_high, flux_u, nt))
+    east_spectra, flux_v = lax.optimization_barrier((east_spectra, flux_v))
+    z_east = exchange(east_spectra)
+    north_spectra = blocks(dot(s_high, flux_v, nt))
+    north_spectra, c_flat, w_flat, u_bf, v_bf = lax.optimization_barrier(
+        (north_spectra, c_flat, w_flat, u_bf, v_bf)
+    )
+    z_north = exchange(north_spectra)
+    c_below = lax.ppermute(c_flat, "gz", up)
 
     first_row = strip * row_count
     rows = lambda t: lax.dynamic_slice_in_dim(t, first_row, row_count, 1)
@@ -199,7 +206,6 @@
     rhs_part = three(y_high, y_low, a_modes) + three(s_high, s_low, b_modes)
     low_part = three(y_high, y_low, w_modes)
     got = exchange(blocks(jnp.concatenate([rhs_part, low_part], axis=1)))
-    z_north = exchange(blocks(dot(s_high, flux_v, nt)))
 
     tracer = c_flat.astype(F32)
     flux = w_flat.astype(F32) * (tracer + c_below.astype(F32)) * (0.5 / LEVEL_STEP)

time: 167 us -> 157 us (0.940)
  local copies, waits for them, and re-layouts: 21.5 us -> 8.71 us
  matrix products: 55.8 us -> 58.9 us
  Pallas kernels: 4.48 us -> 7.58 us
  waiting for transfers between devices: 13.8 us -> 16.9 us
  other arithmetic: 12.3 us -> 9.9 us
  blocking collectives: 30.5 us -> 28.8 us
    unnamed x70 -> x52, local copies, waits for them, and re-layouts: 11.2 us -> 0.87 us
    pallas_call x1, Pallas kernels: 4.48 us -> 7.58 us  [drag_fields(): pl.pallas_call(drag_kernel, grid=(rows // block,), in_specs=[small] * 3 +...]
    dot_general x20, matrix products: 55.8 us -> 58.9 us  [dot(): return lax.dot_general(a, b, (dims, ((), ())), preferred_element_type=F32)]
    all_to_all x2, waiting for transfers between devices: 1.28 us -> 4.24 us  [the longest x1 4.24 us: per_device(): z_east = exchange(east_spectra)]
    all_gather x1, blocking collectives: 15.5 us -> 13.8 us  [per_device(): all_sums = lax.all_gather(sums, 'gz', axis=0, tiled=False)]
  transfers between devices with their start and end apart: 6 -> 6, of which waited for: 2 -> 2; matrix products, arithmetic and copies ran while one was open for 46% -> 42% of each run, Pallas kernels for 3% -> 0%
where the time goes in v3:
time: 157 us; the launch traced here: 156 us
  matrix products  58.9 us (38%)
  blocking collectives  28.8 us (18%)
  starting transfers between devices  24.3 us (15%)
  waiting for transfers between devices  16.9 us (11%)
  other arithmetic  9.9 us (6%)
  local copies, waits for them, and re-layouts  8.71 us (6%)
  Pallas kernels  7.58 us (5%)
    dot_general x20, matrix products, dot(): return lax.dot_general(a, b, (dims, ((), ())), preferred_element_type=F32)  58.9 us
    all_gather x1, blocking collectives, per_device(): solved = lax.all_gather(own.astype(BF), 'xy', axis=0, tiled=True)  15 us
    all_gather x1, blocking collectives, per_device(): all_sums = lax.all_gather(sums, 'gz', axis=0, tiled=False)  13.8 us
    all_to_all x1, waiting for transfers between devices, per_device(): got = exchange(blocks(jnp.concatenate([rhs_part, low_part], axis=1)))  12.7 us
    pallas_call x1, Pallas kernels, drag_fields(): pl.pallas_call(drag_kernel, grid=(rows // block,), in_specs=[small] * 3 +...  7.58 us
    all_to_all x1, starting transfers between devices, per_device(): z_north = exchange(north_spectra)  6.46 us
    all_to_all x1, starting transfers between devices, per_device(): z_east = exchange(east_spectra)  5.08 us
    ppermute x1, starting transfers between devices, per_device(): c_below = lax.ppermute(c_flat, 'gz', up)  4.4 us
  transfers between devices with their start and end apart: 6, of which 2 were waited for; matrix products, arithmetic and copies ran while one was open for 42% of the time, Pallas kernels for 0%

profile of v3, /device:TPU:0, one launch (start us, length us, event | category | flops | bytes accessed | tf_op | source)
XLA Modules:
  0.0 156.4 jit_solution(6915566914555408961)
XLA Ops:
  0.7 7.6 %shard_map.239 = (bf16[256,2048]{1,0:T(8,128)(2,1)}, bf16[256,2048]{1,0:T(8,128)(2,1)}, bf16[256,2048]{1,0:T(8,128)(2,1)}, bf16[256,2048]{1,0:T(8,128)(2,1)}, f32[256,2048]{1,0:T(8,128)}) custom-call(s32[1]{0:T(128)} %bitcast.level, f32[8]{0:T(128)} %area.1, f32[8]{0:T(128)} %wall_heat.1, bf16[256,2048]{1,0:T(8,128)(2,1)} %bitcast.119, ...), custom_call_target="tpu_custom_call" | custom-call | flops 31457280 | bytes 13631488 | tf_op jit(solution)/shard_map/pallas_call | solution.py:149
  8.2 5.5 %convolution_convert_fusion.1 = bf16[256,1344]{0,1:T(8,128)(2,1)} fusion(bf16[256,2048]{1,0:T(8,128)(2,1)} %get-tuple-element.15, bf16[1344,2048]{1,0:T(8,128)(2,1)} %constant.92.clone), kind=kOutput, calls=%fused_computation.4 | convolution fusion | flops 1409630208 | bytes 7241728 | tf_op jit(solution)/shard_map/dot_general | solution.py:113
  13.8 2.5 %convolution_convert_fusion = bf16[256,1344]{0,1:T(8,128)(2,1)} fusion(bf16[256,2048]{1,0:T(8,128)(2,1)S(1)} %copy-done.14, bf16[1344,2048]{1,0:T(8,128)(2,1)S(1)} %bitcast.101), kind=kOutput, calls=%fused_computation.3 | convolution fusion | flops 1409630208 | bytes 7241728 | tf_op jit(solution)/shard_map/dot_general | solution.py:113
  16.3 6.5 %all-to-all-start.1 = ((bf16[8,168,256]{2,1,0:T(8,128)(2,1)}), bf16[8,168,256]{2,1,0:T(8,128)(2,1)}, u32[]{:S(2)}, u32[]{:S(2)}) async-start(bf16[8,168,256]{2,1,0:T(8,128)(2,1)} %bitcast.8), calls=%async_computation.1 | async-start | bytes 1376256 | tf_op jit(solution)/shard_map/all_to_all | solution.py:190
  22.8 4.4 %collective-permute-start = (bf16[256,2048]{1,0:T(8,128)(2,1)S(1)}, bf16[256,2048]{1,0:T(8,128)(2,1)}, u32[]{:S(2)}, u32[]{:S(2)}) collective-permute-start(bf16[256,2048]{1,0:T(8,128)(2,1)S(1)} %bitcast.105), channel_id=1, source_target_pairs={{0,8},{8,16},{16,24},{1,9},{9,17},{17,25},{2,10},{10,18},{18,26},{... | collective-permute-start | bytes 3145736 | tf_op jit(solution)/shard_map/ppermute | solution.py:191
  29.2 2.2 %convolution_multiply_fusion.1 = f32[136,2048]{1,0:T(8,128)S(1)} fusion(bf16[256,2048]{1,0:T(8,128)(2,1)} %bitcast.114, bf16[136,256]{1,0:T(8,128)(2,1)S(1)} %get-tuple-element.40, bf16[136,256]{1,0:T(8,128)(2,1)S(1)} %get-tuple-element.41), kind=kOutput, calls=%fused_computation.5 | convolution fusion | flops 289964032 | bytes 2301952 | tf_op jit(solution)/shard_map/dot_general | solution.py:113
  44.6 2.8 %fusion.5 = bf16[1344,136]{0,1:T(8,128)(2,1)} fusion(f32[136,1344]{1,0:T(8,128)S(1)} %convolution_add_fusion.4, f32[136,1344]{1,0:T(8,128)S(1)} %convolution_add_fusion.3, bf16[1344,2048]{1,0:T(8,128)(2,1)S(1)} %bitcast.109, f32[136,2048]{1,0:T(8,128)S(1)} %fusion.12), kind=kOutput, calls=%fused_computation.19 | convolution fusion | flops 749788672 | bytes 8446976 | tf_op jit(solution)/shard_map/dot_general | solution.py:113
  47.4 3.1 %convolution_add_fusion.1 = f32[136,1344]{1,0:T(8,128)} fusion(f32[136,1344]{1,0:T(8,128)S(1)} %fusion.32, bf16[1344,2048]{1,0:T(8,128)(2,1)S(1)} %bitcast.97, f32[136,2048]{1,0:T(8,128)S(1)} %convolution_multiply_fusion.1), kind=kOutput, calls=%fused_computation.8 | convolution fusion | flops 749701632 | bytes 8081408 | tf_op jit(solution)/shard_map/dot_general | solution.py:113
  50.4 5.1 %all-to-all-start = ((bf16[8,168,256]{2,1,0:T(8,128)(2,1)}), bf16[8,168,256]{2,1,0:T(8,128)(2,1)}, u32[]{:S(2)}, u32[]{:S(2)}) async-start(bf16[8,168,256]{2,1,0:T(8,128)(2,1)} %bitcast.121), calls=%async_computation | async-start | bytes 1376256 | tf_op jit(solution)/shard_map/all_to_all | solution.py:185
  55.5 5.5 %fusion.4 = bf16[1344,136]{0,1:T(8,128)(2,1)} fusion(f32[136,1344]{1,0:T(8,128)} %convolution_add_fusion.1, bf16[1344,2048]{1,0:T(8,128)(2,1)} %constant.98.clone, f32[136,2048]{1,0:T(8,128)S(1)} %convolution_multiply_fusion.1), kind=kOutput, calls=%fused_computation.18 | convolution fusion | flops 749605888 | bytes 7715840 | tf_op jit(solution)/shard_map/dot_general | solution.py:113
  65.1 2.7 %fusion.21 = bf16[256,2048]{1,0:T(8,128)(2,1)} fusion(bf16[256,2048]{1,0:T(8,128)(2,1)} %collective-permute-done, bf16[256,2048]{1,0:T(8,128)(2,1)S(1)} %bitcast.106, bf16[256,2048]{1,0:T(8,128)(2,1)S(1)} %bitcast.115), kind=kLoop, calls=%fused_computation.47 | loop fusion | flops 3670016 | bytes 4194304 | tf_op jit(solution)/shard_map/convert_element_type | solution.py:212
  70.3 4.2 %all-to-all-done = bf16[8,168,256]{2,1,0:T(8,128)(2,1)} async-done(((bf16[8,168,256]{2,1,0:T(8,128)(2,1)}), bf16[8,168,256]{2,1,0:T(8,128)(2,1)}, u32[]{:S(2)}, u32[]{:S(2)}) %all-to-all-start) | async-done | bytes 688160 | tf_op jit(solution)/shard_map/all_to_all | solution.py:185
  74.5 3.6 %all-to-all-start.3 = ((bf16[8,168,272]{2,1,0:T(8,128)(2,1)}), bf16[8,168,272]{2,1,0:T(8,128)(2,1)S(1)}, u32[]{:S(2)}, u32[]{:S(2)}) async-start(bf16[8,168,272]{2,1,0:T(8,128)(2,1)} %bitcast.17), calls=%async_computation.3 | async-start | bytes 2064384 | tf_op jit(solution)/shard_map/all_to_all | solution.py:208
  79.2 5.0 %fusion.66 = f32[168,2048]{1,0:T(8,128)S(1)} fusion(bf16[168,2048]{1,0:T(8,128)(2,1)S(1)} %bitcast.112, bf16[2048,2048]{1,0:T(8,128)(2,1)} %constant.105.clone), kind=kOutput, calls=%fused_computation.119 | convolution fusion | flops 1409286144 | bytes 10452992 | tf_op jit(solution)/shard_map/dot_general | solution.py:113
  84.3 5.0 %convolution_add_fusion.6 = f32[168,2048]{1,0:T(8,128)S(1)} fusion(f32[168,2048]{1,0:T(8,128)S(1)} %fusion.66, bf16[168,2048]{1,0:T(8,128)(2,1)S(1)} %bitcast.113, bf16[2048,2048]{1,0:T(8,128)(2,1)} %constant.106.clone), kind=kOutput, calls=%fused_computation.14 | convolution fusion | flops 1409630208 | bytes 11829248 | tf_op jit(solution)/shard_map/dot_general | solution.py:113
  91.5 12.7 %all-to-all-done.3 = bf16[8,168,272]{2,1,0:T(8,128)(2,1)S(1)} async-done(((bf16[8,168,272]{2,1,0:T(8,128)(2,1)}), bf16[8,168,272]{2,1,0:T(8,128)(2,1)S(1)}, u32[]{:S(2)}, u32[]{:S(2)}) %all-to-all-start.3) | async-done | bytes 731168 | tf_op jit(solution)/shard_map/all_to_all | solution.py:208
  104.2 3.5 %all-to-all-start.2 = ((bf16[8,168,256]{2,1,0:T(8,128)(2,1)}), bf16[8,168,256]{2,1,0:T(8,128)(2,1)S(1)}, u32[]{:S(2)}, u32[]{:S(2)}) async-start(bf16[8,168,256]{2,1,0:T(8,128)(2,1)} %bitcast.118), calls=%async_computation.2 | async-start | bytes 1376256 | tf_op jit(solution)/shard_map/all_to_all | solution.py:267
  108.0 13.8 %all-gather = f32[672,272]{1,0:T(8,128)S(1)} all-gather(f32[168,272]{1,0:T(8,128)S(1)} %convert_reduce_fusion), channel_id=2, replica_groups=mesh['gz'=4,'xy'=8] {'gz'}, dimensions={0}, use_global_device_ids=true | all-gather | bytes 913920 | tf_op jit(solution)/shard_map/all_gather | solution.py:215
  122.8 15.0 %all-gather.1 = bf16[8,168,136]{1,2,0:T(8,128)(2,1)S(1)} all-gather(bf16[1,168,136]{1,2,0:T(8,128)(2,1)S(1)} %copy.55), channel_id=1, replica_groups=mesh['gz'=4,'xy'=8] {'xy'}, dimensions={0}, use_global_device_ids=true | all-gather | bytes 411264 | tf_op jit(solution)/shard_map/all_gather | solution.py:268
  138.4 3.6 %fusion.67 = f32[136,2048]{1,0:T(8,128)S(1)} fusion(bf16[1344,136]{0,1:T(8,128)(2,1)S(1)} %reshape.80, bf16[1344,2048]{1,0:T(8,128)(2,1)} %constant.92.clone), kind=kOutput, calls=%fused_computation.120 | convolution fusion | flops 748683264 | bytes 6984704 | tf_op jit(solution)/shard_map/dot_general | solution.py:113
  142.0 3.7 %reduce-precision_convert_fusion = (bf16[136,2048]{1,0:T(8,128)(2,1)S(1)}, bf16[136,2048]{1,0:T(8,128)(2,1)S(1)}) fusion(f32[136,2048]{1,0:T(8,128)S(1)} %fusion.67, bf16[1344,136]{0,1:T(8,128)(2,1)S(1)} %reshape.80, bf16[1344,2048]{1,0:T(8,128)(2,1)} %constant.98.clone), kind=kOutput, calls=%fused_computation.39 | convolution fusion | flops 750075904 | bytes 8098816 | tf_op jit(solution)/shard_map/dot_general | solution.py:113
  145.8 2.1 %fusion = f32[1,256,2048]{2,1,0:T(8,128)} fusion(bf16[136,2048]{1,0:T(8,128)(2,1)S(1)} %get-tuple-element.33, bf16[136,2048]{1,0:T(8,128)(2,1)S(1)} %get-tuple-element.32, bf16[136,256]{1,0:T(8,128)(2,1)S(1)} %copy-done.4, bf16[136,256]{1,0:T(8,128)(2,1)S(1)} %get-tuple-element.40), kind=kOutput, calls=%fused_computation.1 | convolution fusion | flops 433983488 | bytes 3350528 | tf_op jit(solution)/shard_map/dot_general | solution.py:113
  147.9 5.1 %convolution_subtract_fusion = f32[256,2048]{1,0:T(8,128)S(1)} fusion(f32[256,2048]{1,0:T(8,128)} %get-tuple-element.14, bf16[1344,256]{1,0:T(8,128)(2,1)S(1)} %bitcast.110, bf16[1344,2048]{1,0:T(8,128)(2,1)} %constant.92.clone), kind=kOutput, calls=%fused_computation.2 | convolution fusion | flops 1409810432 | bytes 10387456 | tf_op jit(solution)/shard_map/dot_general | solution.py:113
  153.0 3.4 %fusion.26 = bf16[1,256,2048]{2,1,0:T(8,128)(2,1)} fusion(f32[256,2048]{1,0:T(8,128)S(1)} %convolution_subtract_fusion, bf16[256,2048]{1,0:T(8,128)(2,1)} %collective-permute-done, bf16[256,2048]{1,0:T(8,128)(2,1)S(1)} %bitcast.107, bf16[256,2048]{1,0:T(8,128)(2,1)S(1)} %bitcast.116, bf16[256,2048]{1,0:T(8,128)(2,1)} %collective-permute-done.1), kind=kLoop, calls=%fused_computation.52 | loop fusion | flops 5242880 | bytes 7340032 | tf_op jit(solution)/shard_map/broadcast_in_dim | solution.py:280
  (93 shorter events, 26.7 us)
Async XLA Ops:
  0.6 13.1 %slice-start.4 = ((s8[5505024]{0:T(1024)(128)(4,1)}), s8[1310720]{0:T(1024)(128)(4,1)S(1)}, s32[]{:S(2)}) async-start(s8[5505024]{0:T(1024)(128)(4,1)} %bitcast.100), calls=%async_computation.8 | async-start | bytes 2621440
  8.2 5.5 %slice-start.5 = ((s8[5505024]{0:T(1024)(128)(4,1)}), s8[4194304]{0:T(1024)(128)(4,1)S(1)}, s32[]{:S(2)}) async-start(s8[5505024]{0:T(1024)(128)(4,1)} %bitcast.100), calls=%async_computation.9 | async-start | bytes 8388608
  8.2 5.5 %copy-start.14 = (bf16[256,2048]{1,0:T(8,128)(2,1)S(1)}, bf16[256,2048]{1,0:T(8,128)(2,1)}, u32[]{:S(2)}) copy-start(bf16[256,2048]{1,0:T(8,128)(2,1)} %get-tuple-element.18) | copy-start | bytes 3145732
  13.8 9.0 %copy-start = (bf16[1,256,2048]{2,1,0:T(8,128)(2,1)S(1)}, bf16[1,256,2048]{2,1,0:T(8,128)(2,1)}, u32[]{:S(2)}) copy-start(bf16[1,256,2048]{2,1,0:T(8,128)(2,1)} %param.27) | copy-start | bytes 3145732
  16.3 15.5 %slice-start = ((s8[5505024]{0:T(1024)(128)(4,1)}), s8[1310720]{0:T(1024)(128)(4,1)S(1)}, s32[]{:S(2)}) async-start(s8[5505024]{0:T(1024)(128)(4,1)} %bitcast.96), calls=%async_computation.4 | async-start | bytes 2621440
  16.3 34.2 %all-to-all-start.1 = ((bf16[8,168,256]{2,1,0:T(8,128)(2,1)}), bf16[8,168,256]{2,1,0:T(8,128)(2,1)}, u32[]{:S(2)}, u32[]{:S(2)}) async-start(bf16[8,168,256]{2,1,0:T(8,128)(2,1)} %bitcast.8), calls=%async_computation.1 | async-start | bytes 1376256 | tf_op jit(solution)/shard_map/all_to_all | solution.py:190
  22.8 42.3 %collective-permute-start = (bf16[256,2048]{1,0:T(8,128)(2,1)S(1)}, bf16[256,2048]{1,0:T(8,128)(2,1)}, u32[]{:S(2)}, u32[]{:S(2)}) collective-permute-start(bf16[256,2048]{1,0:T(8,128)(2,1)S(1)} %bitcast.105), channel_id=1, source_target_pairs={{0,8},{8,16},{16,24},{1,9},{9,17},{17,25},{2,10},{10,18},{18,26},{... | collective-permute-start | bytes 3145736 | tf_op jit(solution)/shard_map/ppermute | solution.py:191
  27.2 4.2 %copy-start.13 = (bf16[256,2048]{1,0:T(8,128)(2,1)S(1)}, bf16[256,2048]{1,0:T(8,128)(2,1)}, u32[]{:S(2)}) copy-start(bf16[256,2048]{1,0:T(8,128)(2,1)} %get-tuple-element.24) | copy-start | bytes 3145732
  28.2 7.8 %copy-start.3 = (bf16[136,256]{1,0:T(8,128)(2,1)}, bf16[136,256]{1,0:T(8,128)(2,1)S(1)}, u32[]{:S(2)}) copy-start(bf16[136,256]{1,0:T(8,128)(2,1)S(1)} %get-tuple-element.41) | copy-start | bytes 208900
  32.0 4.5 %slice-start.6 = ((s8[5505024]{0:T(1024)(128)(4,1)}), s8[4194304]{0:T(1024)(128)(4,1)S(1)}, s32[]{:S(2)}) async-start(s8[5505024]{0:T(1024)(128)(4,1)} %bitcast.102), calls=%async_computation.10 | async-start | bytes 8388608
  38.6 6.0 %slice-start.8 = ((s8[5505024]{0:T(1024)(128)(4,1)}), s8[4194304]{0:T(1024)(128)(4,1)S(1)}, s32[]{:S(2)}) async-start(s8[5505024]{0:T(1024)(128)(4,1)} %bitcast.108), calls=%async_computation.12 | async-start | bytes 8388608
  50.4 24.1 %all-to-all-start = ((bf16[8,168,256]{2,1,0:T(8,128)(2,1)}), bf16[8,168,256]{2,1,0:T(8,128)(2,1)}, u32[]{:S(2)}, u32[]{:S(2)}) async-start(bf16[8,168,256]{2,1,0:T(8,128)(2,1)} %bitcast.121), calls=%async_computation | async-start | bytes 1376256 | tf_op jit(solution)/shard_map/all_to_all | solution.py:185
  61.0 4.1 %copy-start.1 = (bf16[1,256,2048]{2,1,0:T(8,128)(2,1)S(1)}, bf16[1,256,2048]{2,1,0:T(8,128)(2,1)}, u32[]{:S(2)}) copy-start(bf16[1,256,2048]{2,1,0:T(8,128)(2,1)} %param.26) | copy-start | bytes 3145732
  67.8 85.2 %collective-permute-start.1 = (bf16[256,2048]{1,0:T(8,128)(2,1)}, bf16[256,2048]{1,0:T(8,128)(2,1)}, u32[]{:S(2)}, u32[]{:S(2)}) collective-permute-start(bf16[256,2048]{1,0:T(8,128)(2,1)} %fusion.21), channel_id=1, source_target_pairs={{8,0},{16,8},{24,16},{9,1},{17,9},{25,17},{10,2},{18,10},{26,18},{... | collective-permute-start | bytes 3145736 | tf_op jit(solution)/shard_map/ppermute | solution.py:212
  74.5 29.7 %all-to-all-start.3 = ((bf16[8,168,272]{2,1,0:T(8,128)(2,1)}), bf16[8,168,272]{2,1,0:T(8,128)(2,1)S(1)}, u32[]{:S(2)}, u32[]{:S(2)}) async-start(bf16[8,168,272]{2,1,0:T(8,128)(2,1)} %bitcast.17), calls=%async_computation.3 | async-start | bytes 2064384 | tf_op jit(solution)/shard_map/all_to_all | solution.py:208
  84.2 5.1 %copy-start.5 = (f32[8,256]{1,0:T(8,128)S(1)}, f32[8,256]{1,0:T(8,128)}, u32[]{:S(2)}) copy-start(f32[8,256]{1,0:T(8,128)} %constant.113) | copy-start | bytes 24580
  84.3 5.1 %copy-start.6 = (f32[8,256]{1,0:T(8,128)S(1)}, f32[8,256]{1,0:T(8,128)}, u32[]{:S(2)}) copy-start(f32[8,256]{1,0:T(8,128)} %constant.115) | copy-start | bytes 24580
  84.3 6.0 %copy-start.7 = (f32[2048]{0:T(1024)S(1)}, f32[2048]{0:T(1024)}, u32[]{:S(2)}) copy-start(f32[2048]{0:T(1024)} %constant.116) | copy-start | bytes 24580
  84.3 6.0 %copy-start.8 = (f32[2048]{0:T(1024)S(1)}, f32[2048]{0:T(1024)}, u32[]{:S(2)}) copy-start(f32[2048]{0:T(1024)} %constant.117) | copy-start | bytes 24580
  91.5 30.3 %copy-start.11 = (f32[136]{0:T(256)S(1)}, f32[136]{0:T(256)}, u32[]{:S(2)}) copy-start(f32[136]{0:T(256)} %constant.119) | copy-start | bytes 1636
  104.2 43.6 %all-to-all-start.2 = ((bf16[8,168,256]{2,1,0:T(8,128)(2,1)}), bf16[8,168,256]{2,1,0:T(8,128)(2,1)S(1)}, u32[]{:S(2)}, u32[]{:S(2)}) async-start(bf16[8,168,256]{2,1,0:T(8,128)(2,1)} %bitcast.118), calls=%async_computation.2 | async-start | bytes 1376256 | tf_op jit(solution)/shard_map/all_to_all | solution.py:267
  107.8 14.5 %copy-start.10 = (f32[2,2]{1,0:T(2,128)S(1)}, f32[2,2]{1,0:T(2,128)}, u32[]{:S(2)}) copy-start(f32[2,2]{1,0:T(2,128)} %constant.102.clone) | copy-start | bytes 52
  107.8 14.8 %copy-start.9 = (f32[136]{0:T(256)S(1)}, f32[136]{0:T(256)}, u32[]{:S(2)}) copy-start(f32[136]{0:T(256)} %constant.104.clone) | copy-start | bytes 1636
  147.9 5.1 %copy-start.2 = (bf16[1,256,2048]{2,1,0:T(8,128)(2,1)S(1)}, bf16[1,256,2048]{2,1,0:T(8,128)(2,1)}, u32[]{:S(2)}) copy-start(bf16[1,256,2048]{2,1,0:T(8,128)(2,1)} %param.26) | copy-start | bytes 3145732
  (7 other events, 21.2 us)

commit v4 on v3

--- a/solution.py
+++ b/solution.py
@@ -181,13 +181,13 @@
     exchange = partial(lax.all_to_all, axis_name="xy", split_axis=0, concat_axis=0, tiled=True)
     blocks = lambda t: t.reshape(strips, share, -1).astype(BF)
     east_spectra = blocks(dot(y_high, flux_u, nt))
-    east_spectra, flux_v = lax.optimization_barrier((east_spectra, flux_v))
-    z_east = exchange(east_spectra)
     north_spectra = blocks(dot(s_high, flux_v, nt))
-    north_spectra, c_flat, w_flat, u_bf, v_bf = lax.optimization_barrier(
-        (north_spectra, c_flat, w_flat, u_bf, v_bf)
+    spectra = jnp.concatenate([east_spectra, north_spectra], axis=-1)
+    spectra, c_flat, w_flat, u_bf, v_bf = lax.optimization_barrier(
+        (spectra, c_flat, w_flat, u_bf, v_bf)
     )
-    z_north = exchange(north_spectra)
+    spectra = exchange(spectra)
+    z_east, z_north = spectra[..., :row_count], spectra[..., row_count:]
     c_below = lax.ppermute(c_flat, "gz", up)
 
     first_row = strip * row_count

time: 157 us -> 215 us (1.37)
  blocking collectives: 28.8 us -> 97.1 us
  starting transfers between devices: 24.3 us -> 13.9 us
  matrix products: 58.9 us -> 50.1 us
  local copies, waits for them, and re-layouts: 8.71 us -> 13.2 us
  waiting for transfers between devices: 16.9 us -> 20.5 us
    all_to_all x0 -> x1, blocking collectives: none -> 32.6 us  [per_device(): got = exchange(blocks(jnp.concatenate([rhs_part, low_part], axis=1)))]
    all_gather x1, blocking collectives: 13.8 us -> 38 us  [per_device(): all_sums = lax.all_gather(sums, 'gz', axis=0, tiled=False)]
    ppermute x1, waiting for transfers between devices: 0.01 us -> 20.5 us  [per_device(): c_below = lax.ppermute(c_flat, 'gz', up)]
    all_to_all x3 -> x1, waiting for transfers between devices: 16.9 us -> 0.01 us  [per_device(): spectra = exchange(spectra)]
    all_to_all x3 -> x1, starting transfers between devices: 15.1 us -> 3.57 us  [per_device(): spectra = exchange(spectra)]
    all_gather x1, blocking collectives: 15 us -> 26.5 us  [per_device(): solved = lax.all_gather(own.astype(BF), 'xy', axis=0, tiled=True)]
    dot_general x20, matrix products: 58.9 us -> 50.1 us  [dot(): return lax.dot_general(a, b, (dims, ((), ())), preferred_element_type=F32)]
    unnamed x52 -> x58, local copies, waits for them, and re-layouts: 0.87 us -> 3.56 us
  transfers between devices with their start and end apart: 6 -> 4, of which waited for: 2 -> 1; matrix products, arithmetic and copies ran while one was open for 42% -> 17% of each run, Pallas kernels for 0% -> 0%
where the time goes in v4:
time: 215 us; the launch traced here: 214 us
  blocking collectives  97.1 us (45%)
  matrix products  50.1 us (23%)
  waiting for transfers between devices  20.5 us (10%)
  starting transfers between devices  13.9 us (6%)
  local copies, waits for them, and re-layouts  13.2 us (6%)
  other arithmetic  10.4 us (5%)
  Pallas kernels  7.59 us (4%)
    dot_general x20, matrix products, dot(): return lax.dot_general(a, b, (dims, ((), ())), preferred_element_type=F32)  50.1 us
    all_gather x1, blocking collectives, per_device(): all_sums = lax.all_gather(sums, 'gz', axis=0, tiled=False)  38 us
    all_to_all x1, blocking collectives, per_device(): got = exchange(blocks(jnp.concatenate([rhs_part, low_part], axis=1)))  32.6 us
    all_gather x1, blocking collectives, per_device(): solved = lax.all_gather(own.astype(BF), 'xy', axis=0, tiled=True)  26.5 us
    ppermute x1, waiting for transfers between devices, per_device(): c_below = lax.ppermute(c_flat, 'gz', up)  20.5 us
    pallas_call x1, Pallas kernels, drag_fields(): pl.pallas_call(drag_kernel, grid=(rows // block,), in_specs=[small] * 3 +...  7.59 us
    all_to_all x1, starting transfers between devices, per_device(): returned = exchange(back).reshape(strips * share, row_count)  4.53 us
    ppermute x1, starting transfers between devices, per_device(): c_below = lax.ppermute(c_flat, 'gz', up)  4.41 us
  transfers between devices with their start and end apart: 4, of which 1 were waited for; matrix products, arithmetic and copies ran while one was open for 17% of the time, Pallas kernels for 0%

profile of v4, /device:TPU:0, one launch (start us, length us, event | category | flops | bytes accessed | tf_op | source)
XLA Modules:
  0.0 214.2 jit_solution(8742244953206207576)
XLA Ops:
  0.7 7.6 %shard_map.239 = (bf16[256,2048]{1,0:T(8,128)(2,1)}, bf16[256,2048]{1,0:T(8,128)(2,1)}, bf16[256,2048]{1,0:T(8,128)(2,1)}, bf16[256,2048]{1,0:T(8,128)(2,1)}, f32[256,2048]{1,0:T(8,128)}) custom-call(s32[1]{0:T(128)} %bitcast.level, f32[8]{0:T(128)} %area.1, f32[8]{0:T(128)} %wall_heat.1, bf16[256,2048]{1,0:T(8,128)(2,1)} %bitcast.125, ...), custom_call_target="tpu_custom_call" | custom-call | flops 31457280 | bytes 13631488 | tf_op jit(solution)/shard_map/pallas_call | solution.py:149
  8.3 4.7 %convolution_convert_fusion.1 = bf16[256,1344]{0,1:T(8,128)(2,1)S(1)} fusion(bf16[256,2048]{1,0:T(8,128)(2,1)} %get-tuple-element.13, bf16[1344,2048]{1,0:T(8,128)(2,1)} %constant.92.clone), kind=kOutput, calls=%fused_computation.4 | convolution fusion | flops 1409630208 | bytes 7241728 | tf_op jit(solution)/shard_map/dot_general | solution.py:113
  17.3 4.9 %fusion.32 = f32[136,1344]{1,0:T(8,128)S(1)} fusion(bf16[1344,2048]{1,0:T(8,128)(2,1)} %constant.92.clone, f32[136,2048]{1,0:T(8,128)S(1)} %convolution_multiply_fusion.1), kind=kOutput, calls=%fused_computation.66 | convolution fusion | flops 749240320 | bytes 7350272 | tf_op jit(solution)/shard_map/dot_general | solution.py:113
  23.6 2.0 fusion.30
  25.6 2.0 convolution_add_fusion.5
  28.2 2.0 fusion.31
  30.2 2.0 convolution_add_fusion.3
  32.3 2.2 %convolution_add_fusion.1 = f32[136,1344]{1,0:T(8,128)S(1)} fusion(f32[136,1344]{1,0:T(8,128)S(1)} %fusion.32, bf16[1344,2048]{1,0:T(8,128)(2,1)S(1)} %bitcast.101, f32[136,2048]{1,0:T(8,128)S(1)} %convolution_multiply_fusion.1), kind=kOutput, calls=%fused_computation.8 | convolution fusion | flops 749701632 | bytes 8081408 | tf_op jit(solution)/shard_map/dot_general | solution.py:113
  34.5 2.0 convolution_add_fusion.4
  38.5 2.0 fusion.5
  41.8 32.6 %all_to_all.15 = bf16[8,168,272]{2,1,0:T(8,128)(2,1)} all-to-all(bf16[8,168,272]{2,1,0:T(8,128)(2,1)S(1)} %bitcast.123), channel_id=1, replica_groups=mesh['gz'=4,'xy'=8] {'xy'}, dimensions={0} | all-to-all | bytes 1462272 | tf_op jit(solution)/shard_map/all_to_all | solution.py:208
  74.5 3.6 %all-to-all-start = ((bf16[8,168,512]{2,1,0:T(8,128)(2,1)}), bf16[8,168,512]{2,1,0:T(8,128)(2,1)S(1)}, u32[]{:S(2)}, u32[]{:S(2)}) async-start(bf16[8,168,512]{2,1,0:T(8,128)(2,1)} %pad_maximum_fusion), calls=%async_computation | async-start | bytes 2752512 | tf_op jit(solution)/shard_map/all_to_all | solution.py:189
  78.1 4.4 %collective-permute-start = (bf16[256,2048]{1,0:T(8,128)(2,1)S(1)}, bf16[256,2048]{1,0:T(8,128)(2,1)}, u32[]{:S(2)}, u32[]{:S(2)}) collective-permute-start(bf16[256,2048]{1,0:T(8,128)(2,1)S(1)} %bitcast.111), channel_id=1, source_target_pairs={{0,8},{8,16},{16,24},{1,9},{9,17},{17,25},{2,10},{10,18},{18,26},{... | collective-permute-start | bytes 3145736 | tf_op jit(solution)/shard_map/ppermute | solution.py:191
  83.9 20.5 %collective-permute-done = bf16[256,2048]{1,0:T(8,128)(2,1)} collective-permute-done((bf16[256,2048]{1,0:T(8,128)(2,1)S(1)}, bf16[256,2048]{1,0:T(8,128)(2,1)}, u32[]{:S(2)}, u32[]{:S(2)}) %collective-permute-start) | collective-permute-done | bytes 1048608 | tf_op jit(solution)/shard_map/ppermute | solution.py:191
  104.4 2.7 %fusion.21 = bf16[256,2048]{1,0:T(8,128)(2,1)} fusion(bf16[256,2048]{1,0:T(8,128)(2,1)} %collective-permute-done, bf16[256,2048]{1,0:T(8,128)(2,1)S(1)} %bitcast.112, bf16[256,2048]{1,0:T(8,128)(2,1)S(1)} %bitcast.121), kind=kLoop, calls=%fused_computation.48 | loop fusion | flops 3670016 | bytes 4194304 | tf_op jit(solution)/shard_map/convert_element_type | solution.py:212
  108.7 38.0 %all-gather = f32[672,272]{1,0:T(8,128)S(1)} all-gather(f32[168,272]{1,0:T(8,128)S(1)} %convert_reduce_fusion), channel_id=2, replica_groups=mesh['gz'=4,'xy'=8] {'gz'}, dimensions={0}, use_global_device_ids=true | all-gather | bytes 913920 | tf_op jit(solution)/shard_map/all_gather | solution.py:215
  154.0 5.1 %fusion.66 = f32[168,2048]{1,0:T(8,128)S(1)} fusion(bf16[168,2048]{1,0:T(8,128)(2,1)S(1)} %bitcast.118, bf16[2048,2048]{1,0:T(8,128)(2,1)} %constant.105.clone), kind=kOutput, calls=%fused_computation.124 | convolution fusion | flops 1409286144 | bytes 10452992 | tf_op jit(solution)/shard_map/dot_general | solution.py:113
  162.6 4.5 %all-to-all-start.1 = ((bf16[8,168,256]{2,1,0:T(8,128)(2,1)}), bf16[8,168,256]{2,1,0:T(8,128)(2,1)S(1)}, u32[]{:S(2)}, u32[]{:S(2)}) async-start(bf16[8,168,256]{2,1,0:T(8,128)(2,1)} %bitcast.99), calls=%async_computation.1 | async-start | bytes 1376256 | tf_op jit(solution)/shard_map/all_to_all | solution.py:267
  167.3 26.5 %all-gather.1 = bf16[8,168,136]{1,2,0:T(8,128)(2,1)S(1)} all-gather(bf16[1,168,136]{1,2,0:T(8,128)(2,1)S(1)} %copy.55), channel_id=1, replica_groups=mesh['gz'=4,'xy'=8] {'xy'}, dimensions={0}, use_global_device_ids=true | all-gather | bytes 411264 | tf_op jit(solution)/shard_map/all_gather | solution.py:268
  196.3 3.6 %fusion.67 = f32[136,2048]{1,0:T(8,128)S(1)} fusion(bf16[1344,136]{0,1:T(8,128)(2,1)S(1)} %reshape.80, bf16[1344,2048]{1,0:T(8,128)(2,1)} %constant.92.clone), kind=kOutput, calls=%fused_computation.125 | convolution fusion | flops 748683264 | bytes 6984704 | tf_op jit(solution)/shard_map/dot_general | solution.py:113
  200.0 3.7 %reduce-precision_convert_fusion = (bf16[136,2048]{1,0:T(8,128)(2,1)S(1)}, bf16[136,2048]{1,0:T(8,128)(2,1)S(1)}) fusion(f32[136,2048]{1,0:T(8,128)S(1)} %fusion.67, bf16[1344,136]{0,1:T(8,128)(2,1)S(1)} %reshape.80, bf16[1344,2048]{1,0:T(8,128)(2,1)} %constant.98.clone), kind=kOutput, calls=%fused_computation.39 | convolution fusion | flops 750075904 | bytes 8098816 | tf_op jit(solution)/shard_map/dot_general | solution.py:113
  203.7 2.1 fusion
  205.8 5.0 %convolution_subtract_fusion = f32[256,2048]{1,0:T(8,128)S(1)} fusion(f32[256,2048]{1,0:T(8,128)} %get-tuple-element.12, bf16[1344,256]{1,0:T(8,128)(2,1)S(1)} %bitcast.116, bf16[1344,2048]{1,0:T(8,128)(2,1)} %constant.92.clone), kind=kOutput, calls=%fused_computation.2 | convolution fusion | flops 1409810432 | bytes 10387456 | tf_op jit(solution)/shard_map/dot_general | solution.py:113
  210.9 3.4 %fusion.26 = bf16[1,256,2048]{2,1,0:T(8,128)(2,1)} fusion(f32[256,2048]{1,0:T(8,128)S(1)} %convolution_subtract_fusion, bf16[256,2048]{1,0:T(8,128)(2,1)} %collective-permute-done, bf16[256,2048]{1,0:T(8,128)(2,1)S(1)} %bitcast.113, bf16[256,2048]{1,0:T(8,128)(2,1)S(1)} %bitcast.122, bf16[256,2048]{1,0:T(8,128)(2,1)} %collective-permute-done.1), kind=kLoop, calls=%fused_computation.53 | loop fusion | flops 5242880 | bytes 7340032 | tf_op jit(solution)/shard_map/broadcast_in_dim | solution.py:280
  (99 shorter events, 25.6 us)
Async XLA Ops:
  0.6 12.3 %slice-start.4 = ((s8[5505024]{0:T(1024)(128)(4,1)}), s8[1310720]{0:T(1024)(128)(4,1)S(1)}, s32[]{:S(2)}) async-start(s8[5505024]{0:T(1024)(128)(4,1)} %bitcast.104), calls=%async_computation.7 | async-start | bytes 2621440
  8.2 4.7 %slice-start.5 = ((s8[5505024]{0:T(1024)(128)(4,1)}), s8[4194304]{0:T(1024)(128)(4,1)S(1)}, s32[]{:S(2)}) async-start(s8[5505024]{0:T(1024)(128)(4,1)} %bitcast.104), calls=%async_computation.8 | async-start | bytes 8388608
  8.2 4.7 %copy-start.15 = (bf16[256,2048]{1,0:T(8,128)(2,1)S(1)}, bf16[256,2048]{1,0:T(8,128)(2,1)}, u32[]{:S(2)}) copy-start(bf16[256,2048]{1,0:T(8,128)(2,1)} %get-tuple-element.14) | copy-start | bytes 3145732
  16.7 10.9 %copy-start.5 = (bf16[136,256]{1,0:T(8,128)(2,1)}, bf16[136,256]{1,0:T(8,128)(2,1)S(1)}, u32[]{:S(2)}) copy-start(bf16[136,256]{1,0:T(8,128)(2,1)S(1)} %get-tuple-element.41) | copy-start | bytes 208900
  16.8 6.8 %slice-start = ((s8[5505024]{0:T(1024)(128)(4,1)}), s8[4194304]{0:T(1024)(128)(4,1)S(1)}, s32[]{:S(2)}) async-start(s8[5505024]{0:T(1024)(128)(4,1)} %bitcast.100), calls=%async_computation.3 | async-start | bytes 8388608
  17.2 5.8 %copy-start.14 = (bf16[256,2048]{1,0:T(8,128)(2,1)S(1)}, bf16[256,2048]{1,0:T(8,128)(2,1)}, u32[]{:S(2)}) copy-start(bf16[256,2048]{1,0:T(8,128)(2,1)} %get-tuple-element.20) | copy-start | bytes 3145732
  17.2 6.3 %slice-start.1 = ((s8[5505024]{0:T(1024)(128)(4,1)}), s8[1310720]{0:T(1024)(128)(4,1)S(1)}, s32[]{:S(2)}) async-start(s8[5505024]{0:T(1024)(128)(4,1)} %bitcast.100), calls=%async_computation.4 | async-start | bytes 2621440
  23.6 4.6 %slice-start.6 = ((s8[5505024]{0:T(1024)(128)(4,1)}), s8[4194304]{0:T(1024)(128)(4,1)S(1)}, s32[]{:S(2)}) async-start(s8[5505024]{0:T(1024)(128)(4,1)} %bitcast.106), calls=%async_computation.9 | async-start | bytes 8388608
  30.2 4.2 %slice-start.2 = ((s8[5505024]{0:T(1024)(128)(4,1)}), s8[4194304]{0:T(1024)(128)(4,1)S(1)}, s32[]{:S(2)}) async-start(s8[5505024]{0:T(1024)(128)(4,1)} %bitcast.102), calls=%async_computation.5 | async-start | bytes 8388608
  32.3 6.2 %slice-start.10 = ((s8[5505024]{0:T(1024)(128)(4,1)}), s8[4194304]{0:T(1024)(128)(4,1)S(1)}, s32[]{:S(2)}) async-start(s8[5505024]{0:T(1024)(128)(4,1)} %bitcast.114), calls=%async_computation.13 | async-start | bytes 8388608
  34.5 4.0 %slice-start.11 = ((s8[5505024]{0:T(1024)(128)(4,1)}), s8[1310720]{0:T(1024)(128)(4,1)S(1)}, s32[]{:S(2)}) async-start(s8[5505024]{0:T(1024)(128)(4,1)} %bitcast.114), calls=%async_computation.14 | async-start | bytes 2621440
  41.8 36.2 %copy-start = (bf16[1,256,2048]{2,1,0:T(8,128)(2,1)S(1)}, bf16[1,256,2048]{2,1,0:T(8,128)(2,1)}, u32[]{:S(2)}) copy-start(bf16[1,256,2048]{2,1,0:T(8,128)(2,1)} %param.27) | copy-start | bytes 3145732
  74.5 78.4 %all-to-all-start = ((bf16[8,168,512]{2,1,0:T(8,128)(2,1)}), bf16[8,168,512]{2,1,0:T(8,128)(2,1)S(1)}, u32[]{:S(2)}, u32[]{:S(2)}) async-start(bf16[8,168,512]{2,1,0:T(8,128)(2,1)} %pad_maximum_fusion), calls=%async_computation | async-start | bytes 2752512 | tf_op jit(solution)/shard_map/all_to_all | solution.py:189
  78.1 26.4 %collective-permute-start = (bf16[256,2048]{1,0:T(8,128)(2,1)S(1)}, bf16[256,2048]{1,0:T(8,128)(2,1)}, u32[]{:S(2)}, u32[]{:S(2)}) collective-permute-start(bf16[256,2048]{1,0:T(8,128)(2,1)S(1)} %bitcast.111), channel_id=1, source_target_pairs={{0,8},{8,16},{16,24},{1,9},{9,17},{17,25},{2,10},{10,18},{18,26},{... | collective-permute-start | bytes 3145736 | tf_op jit(solution)/shard_map/ppermute | solution.py:191
  83.9 24.7 %copy-start.2 = (bf16[8,168,272]{2,1,0:T(8,128)(2,1)S(1)}, bf16[8,168,272]{2,1,0:T(8,128)(2,1)}, u32[]{:S(2)}) copy-start(bf16[8,168,272]{2,1,0:T(8,128)(2,1)} %all_to_all.15) | copy-start | bytes 2193412
  107.1 39.6 %copy-start.12 = (f32[136]{0:T(256)S(1)}, f32[136]{0:T(256)}, u32[]{:S(2)}) copy-start(f32[136]{0:T(256)} %constant.119) | copy-start | bytes 1636
  107.1 103.7 %collective-permute-start.1 = (bf16[256,2048]{1,0:T(8,128)(2,1)}, bf16[256,2048]{1,0:T(8,128)(2,1)}, u32[]{:S(2)}, u32[]{:S(2)}) collective-permute-start(bf16[256,2048]{1,0:T(8,128)(2,1)} %fusion.21), channel_id=1, source_target_pairs={{8,0},{16,8},{24,16},{9,1},{17,9},{25,17},{10,2},{18,10},{26,18},{... | collective-permute-start | bytes 3145736 | tf_op jit(solution)/shard_map/ppermute | solution.py:212
  147.8 5.3 %copy-start.7 = (f32[8,256]{1,0:T(8,128)S(1)}, f32[8,256]{1,0:T(8,128)}, u32[]{:S(2)}) copy-start(f32[8,256]{1,0:T(8,128)} %constant.113) | copy-start | bytes 24580
  153.9 5.3 %slice-start.8 = ((s8[8388608]{0:T(1024)(128)(4,1)}), s8[4194304]{0:T(1024)(128)(4,1)S(1)}, s32[]{:S(2)}) async-start(s8[8388608]{0:T(1024)(128)(4,1)} %bitcast.108), calls=%async_computation.11 | async-start | bytes 8388608
  154.0 5.7 %slice-start.9 = ((s8[8388608]{0:T(1024)(128)(4,1)}), s8[4194304]{0:T(1024)(128)(4,1)S(1)}, s32[]{:S(2)}) async-start(s8[8388608]{0:T(1024)(128)(4,1)} %bitcast.108), calls=%async_computation.12 | async-start | bytes 8388608
  161.5 5.6 %copy-start.4 = (f32[168,136]{1,0:T(8,128)S(1)}, f32[168,136]{1,0:T(8,128)}, u32[]{:S(2)}) copy-start(f32[168,136]{1,0:T(8,128)} %dynamic_update_slice.7) | copy-start | bytes 274180
  161.5 5.6 %copy-start.11 = (f32[136]{0:T(256)S(1)}, f32[136]{0:T(256)}, u32[]{:S(2)}) copy-start(f32[136]{0:T(256)} %constant.104.clone) | copy-start | bytes 1636
  162.6 43.2 %all-to-all-start.1 = ((bf16[8,168,256]{2,1,0:T(8,128)(2,1)}), bf16[8,168,256]{2,1,0:T(8,128)(2,1)S(1)}, u32[]{:S(2)}, u32[]{:S(2)}) async-start(bf16[8,168,256]{2,1,0:T(8,128)(2,1)} %bitcast.99), calls=%async_computation.1 | async-start | bytes 1376256 | tf_op jit(solution)/shard_map/all_to_all | solution.py:267
  199.9 3.8 %copy-start.6 = (bf16[136,256]{1,0:T(8,128)(2,1)S(1)}, bf16[136,256]{1,0:T(8,128)(2,1)}, u32[]{:S(2)}) copy-start(bf16[136,256]{1,0:T(8,128)(2,1)} %copy-done.5) | copy-start | bytes 208900
  (8 other events, 12.1 us)
